TPU v7x, 32 devices: a whole 2x2x4 slice. The times are simulated.
32 devices in a mesh: ctx: 4 (over z), seq: 2 (over x), wa: 4 (over y, core).
Axes of the slice: x: 2, y: 2, z: 4, core: 2. Of those that a mesh axis runs over, the one named last changes fastest.
Arguments:
- tokens: bfloat16 [8, 768, 4096], P('seq', 'wa', 'ctx'), may hold values from -6 to 6
- first_gain: bfloat16 [768], P('wa'), may hold values from 0.5 to 1.5
- qkv_weight: bfloat16 [3, 768, 768], P(None, 'wa'), may hold values from -0.21875 to 0.21875
- attn_out_weight: bfloat16 [768, 768], P('wa'), may hold values from -6 to 6
- second_gain: bfloat16 [768], P('wa'), may hold values from 0.5 to 1.5
- ffn_in_weight: bfloat16 [2, 1152, 768], P(None, 'wa'), may hold values from -0.21875 to 0.21875
- ffn_out_weight: bfloat16 [1152, 768], P('wa'), may hold values from -0.1875 to 0.1875
- cotangent: bfloat16 [8, 768, 4096], P('seq', 'wa', 'ctx'), may hold values from -6 to 6
Outputs:
- output: bfloat16 [8, 768, 4096], P('seq', 'wa', 'ctx')
- grad_tokens: float32 [8, 768, 4096], P('seq', 'wa', 'ctx')
- grad_first_gain: float32 [768], P('wa')
- grad_qkv: float32 [3, 768, 768], P(None, 'wa')
- grad_attn_out: float32 [768, 768], P('wa')
- grad_second_gain: float32 [768], P('wa')
- grad_ffn_in: float32 [2, 1152, 768], P(None, 'wa')
- grad_ffn_out: float32 [1152, 768], P('wa')
All inputs are finite; a program needn't handle non-finite values.
Results may differ from a plain program's by a relative error of at most 0.023.
Values may be sent and summed in bfloat16 or wider, within the bound.
A program may use at most 320 MiB of HBM per device.

v0:
```python
import math

import jax
import jax.numpy as jnp
from jax import lax
from jax.sharding import PartitionSpec as P

HD = 64


EPSILON = 1e-05
THETA_BASE = 160000.0


def rope_tables(positions, head_size):
    half_size = head_size // 2
    frequency = THETA_BASE ** (-jnp.arange(half_size, dtype=jnp.float32) * 2.0 / head_size)
    angles = positions.astype(jnp.float32)[:, None] * frequency[None, :]
    return (jnp.cos(angles), jnp.sin(angles))


def rotate(values, cosine_table, sine_table):
    half_size = values.shape[-1] // 2
    first_half = values[..., :half_size]
    second_half = values[..., half_size:]
    return jnp.concatenate(
        [
            first_half * cosine_table - second_half * sine_table,
            second_half * cosine_table + first_half * sine_table,
        ],
        axis=-1,
    )


def normalize(rows_in):
    center = rows_in - jnp.mean(rows_in, axis=-1, keepdims=True)
    inverse = lax.rsqrt(jnp.mean(center * center, axis=-1, keepdims=True) + EPSILON)
    return (center * inverse, inverse)


def norm_back(grad_hat, normed_hat, inverse):
    mean_grad = jnp.mean(grad_hat, axis=-1, keepdims=True)
    mean_proj = jnp.mean(grad_hat * normed_hat, axis=-1, keepdims=True)
    return inverse * (grad_hat - mean_grad - normed_hat * mean_proj)


def block_size(length):
    return math.gcd(length, 512)


def scores_of(queries, keys_part, score_scale):
    return (
        jnp.einsum("shqe,shke->shqk", queries, keys_part, preferred_element_type=jnp.float32)
        * score_scale
    )


def softmax_totals(queries, keys_all, score_scale):
    key_block = block_size(keys_all.shape[2])
    stat_shape = queries.shape[:3]

    def softmax_key_step(state_in, block_index):
        run_max, run_sum = state_in
        keys_part = lax.dynamic_slice_in_dim(keys_all, block_index * key_block, key_block, 2)
        scores = scores_of(queries, keys_part, score_scale)
        new_max = jnp.maximum(run_max, jnp.max(scores, axis=-1))
        new_sum = run_sum * jnp.exp(run_max - new_max) + jnp.sum(
            jnp.exp(scores - new_max[..., None]), axis=-1
        )
        return ((new_max, new_sum), None)

    start_state = (jnp.full(stat_shape, -jnp.inf, jnp.float32), jnp.zeros(stat_shape, jnp.float32))
    final_state, unused = lax.scan(
        softmax_key_step, start_state, jnp.arange(keys_all.shape[2] // key_block)
    )
    return final_state[0] + jnp.log(final_state[1])


def attend_values(queries, keys_all, values_all, log_total, score_scale):
    key_block = block_size(keys_all.shape[2])

    def attend_key_step(summed, block_index):
        keys_part = lax.dynamic_slice_in_dim(keys_all, block_index * key_block, key_block, 2)
        values_part = lax.dynamic_slice_in_dim(values_all, block_index * key_block, key_block, 2)
        prob_rows = jnp.exp(
            scores_of(queries, keys_part, score_scale) - log_total[..., None]
        ).astype(jnp.bfloat16)
        added = jnp.einsum(
            "shqk,shke->shqe", prob_rows, values_part, preferred_element_type=jnp.float32
        )
        return (summed + added, None)

    summed, unused = lax.scan(
        attend_key_step,
        jnp.zeros(queries.shape, jnp.float32),
        jnp.arange(keys_all.shape[2] // key_block),
    )
    return summed


def query_side(queries, grad_out_low, keys_all, values_all, log_total, grad_dot, score_scale):
    key_block = block_size(keys_all.shape[2])

    def query_key_step(state_in, block_index):
        grad_query, grad_keys, grad_values = state_in
        keys_part = lax.dynamic_slice_in_dim(keys_all, block_index * key_block, key_block, 2)
        values_part = lax.dynamic_slice_in_dim(values_all, block_index * key_block, key_block, 2)
        prob_rows = jnp.exp(scores_of(queries, keys_part, score_scale) - log_total[..., None])
        grad_prob = jnp.einsum(
            "shqe,shke->shqk", grad_out_low, values_part, preferred_element_type=jnp.float32
        )
        grad_score = (prob_rows * (grad_prob - grad_dot[..., None])).astype(jnp.bfloat16)
        grad_query = grad_query + jnp.einsum(
            "shqk,shke->shqe", grad_score, keys_part, preferred_element_type=jnp.float32
        )
        key_term = jnp.einsum(
            "shqk,shqe->shke", grad_score, queries, preferred_element_type=jnp.float32
        )
        value_term = jnp.einsum(
            "shqk,shqe->shke",
            prob_rows.astype(jnp.bfloat16),
            grad_out_low,
            preferred_element_type=jnp.float32,
        )
        grad_keys = lax.dynamic_update_slice_in_dim(grad_keys, key_term, block_index * key_block, 2)
        grad_values = lax.dynamic_update_slice_in_dim(
            grad_values, value_term, block_index * key_block, 2
        )
        return ((grad_query, grad_keys, grad_values), None)

    key_zeros = jnp.zeros(keys_all.shape, jnp.float32)
    start_state = (jnp.zeros(queries.shape, jnp.float32), key_zeros, key_zeros)
    final_state, unused = lax.scan(
        query_key_step, start_state, jnp.arange(keys_all.shape[2] // key_block)
    )
    return (final_state[0] * score_scale, final_state[1] * score_scale, final_state[2])


def geglu(gate_in, up_in):
    return jax.nn.gelu(gate_in, approximate=False) * up_in


def local(
    tokens,
    first_gain,
    qkv_weight,
    attn_out_weight,
    second_gain,
    ffn_in_weight,
    ffn_out_weight,
    cotangent,
):
    seq_count = tokens.shape[0]
    block_len = tokens.shape[2]
    model_width = qkv_weight.shape[2]
    local_width = qkv_weight.shape[1]
    head_count = local_width // HD
    rows_total = seq_count * block_len
    score_scale = 1.0 / math.sqrt(HD)
    shard_width = model_width // lax.axis_size("wa")
    shard_start = lax.axis_index("wa") * shard_width
    qkv_heads = qkv_weight.reshape(3, head_count, HD, model_width)
    attn_heads = attn_out_weight.reshape(head_count, HD, model_width)
    full_tokens, full_cot, gain_one, gain_two = (
        lax.all_gather(tokens, "wa", axis=1, tiled=True),
        lax.all_gather(cotangent, "wa", axis=1, tiled=True),
        lax.all_gather(first_gain, "wa", axis=0, tiled=True),
        lax.all_gather(second_gain, "wa", axis=0, tiled=True),
    )
    gain_one_f = gain_one.astype(jnp.float32)
    gain_two_f = gain_two.astype(jnp.float32)
    inputs = full_tokens.astype(jnp.float32).transpose(0, 2, 1).reshape(rows_total, model_width)
    hat_one, inv_one = normalize(inputs)
    normed_one = (hat_one * gain_one_f).astype(jnp.bfloat16)
    normed_seq = normed_one.reshape(seq_count, block_len, model_width)
    projected = jnp.einsum(
        "sbd,khed->kshbe", normed_seq, qkv_heads, preferred_element_type=jnp.float32
    )
    positions = lax.axis_index("ctx") * block_len + jnp.arange(block_len, dtype=jnp.int32)
    cosine_table, sine_table = rope_tables(positions, HD)
    queries = rotate(projected[0], cosine_table, sine_table).astype(jnp.bfloat16)
    keys_own = rotate(projected[1], cosine_table, sine_table).astype(jnp.bfloat16)
    values_own = projected[2].astype(jnp.bfloat16)
    keys_all, values_all = (
        lax.all_gather(keys_own, "ctx", axis=2, tiled=True),
        lax.all_gather(values_own, "ctx", axis=2, tiled=True),
    )
    log_total = softmax_totals(queries, keys_all, score_scale)
    attended = attend_values(queries, keys_all, values_all, log_total, score_scale)
    attended_low = attended.astype(jnp.bfloat16)
    attn_part = jnp.einsum(
        "shbe,hed->sbd", attended_low, attn_heads, preferred_element_type=jnp.float32
    ).reshape(rows_total, model_width)
    middle = inputs + lax.psum(attn_part.astype(jnp.bfloat16), "wa").astype(jnp.float32)
    hat_two, inv_two = normalize(middle)
    normed_two = (hat_two * gain_two_f).astype(jnp.bfloat16)
    gate_up = jnp.einsum(
        "td,kfd->tkf", normed_two, ffn_in_weight, preferred_element_type=jnp.float32
    )
    mixed, pull_gelu = jax.vjp(geglu, gate_up[:, 0], gate_up[:, 1])
    hidden = mixed.astype(jnp.bfloat16)
    ffn_part = jnp.einsum(
        "stf,fd->sdt",
        hidden.reshape(seq_count, block_len, -1),
        ffn_out_weight,
        preferred_element_type=jnp.float32,
    )
    middle_own = lax.dynamic_slice_in_dim(
        middle.reshape(seq_count, block_len, model_width), shard_start, shard_width, 2
    ).transpose(0, 2, 1)
    ffn_own = lax.psum_scatter(
        ffn_part.astype(jnp.bfloat16), "wa", scatter_dimension=1, tiled=True
    ).astype(jnp.float32)
    output = (middle_own + ffn_own).astype(jnp.bfloat16)
    grad_out = full_cot.transpose(0, 2, 1).reshape(rows_total, model_width)
    grad_ffn_out = jnp.einsum("tf,td->fd", hidden, grad_out, preferred_element_type=jnp.float32)
    grad_hidden = jnp.einsum(
        "td,fd->tf", grad_out, ffn_out_weight, preferred_element_type=jnp.float32
    )
    grad_gate, grad_up = pull_gelu(grad_hidden)
    grad_gate_up = jnp.stack([grad_gate, grad_up], axis=1).astype(jnp.bfloat16)
    grad_ffn_in = jnp.einsum(
        "tkf,td->kfd", grad_gate_up, normed_two, preferred_element_type=jnp.float32
    )
    grad_normed_two = lax.psum(
        jnp.einsum(
            "tkf,kfd->td", grad_gate_up, ffn_in_weight, preferred_element_type=jnp.float32
        ).astype(jnp.bfloat16),
        "wa",
    ).astype(jnp.float32)
    gain_two_grad = jnp.sum(grad_normed_two * hat_two, axis=0)
    grad_middle = grad_out.astype(jnp.float32) + norm_back(
        grad_normed_two * gain_two_f, hat_two, inv_two
    )
    grad_middle_low = grad_middle.astype(jnp.bfloat16).reshape(seq_count, block_len, model_width)
    grad_attn_out = jnp.einsum(
        "shbe,sbd->hed", attended_low, grad_middle_low, preferred_element_type=jnp.float32
    ).reshape(local_width, model_width)
    grad_attended = jnp.einsum(
        "sbd,hed->shbe", grad_middle_low, attn_heads, preferred_element_type=jnp.float32
    ).astype(jnp.bfloat16)
    grad_dot = jnp.sum(grad_attended.astype(jnp.float32) * attended, axis=-1)
    grad_query, grad_keys_all, grad_values_all = query_side(
        queries, grad_attended, keys_all, values_all, log_total, grad_dot, score_scale
    )
    grad_key, grad_value = (
        lax.psum_scatter(
            grad_keys_all.astype(jnp.bfloat16), "ctx", scatter_dimension=2, tiled=True
        ).astype(jnp.float32),
        lax.psum_scatter(
            grad_values_all.astype(jnp.bfloat16), "ctx", scatter_dimension=2, tiled=True
        ).astype(jnp.float32),
    )
    grad_query_raw = rotate(grad_query, cosine_table, -sine_table)
    grad_key_raw = rotate(grad_key, cosine_table, -sine_table)
    grad_projected = jnp.stack([grad_query_raw, grad_key_raw, grad_value], axis=0).astype(
        jnp.bfloat16
    )
    grad_qkv = jnp.einsum(
        "kshbe,sbd->khed", grad_projected, normed_seq, preferred_element_type=jnp.float32
    ).reshape(3, local_width, model_width)
    grad_normed_one = lax.psum(
        jnp.einsum("kshbe,khed->sbd", grad_projected, qkv_heads, preferred_element_type=jnp.float32)
        .reshape(rows_total, model_width)
        .astype(jnp.bfloat16),
        "wa",
    ).astype(jnp.float32)
    gain_one_grad = jnp.sum(grad_normed_one * hat_one, axis=0)
    grad_inputs = grad_middle + norm_back(grad_normed_one * gain_one_f, hat_one, inv_one)
    grad_tokens = lax.dynamic_slice_in_dim(
        grad_inputs.reshape(seq_count, block_len, model_width), shard_start, shard_width, 2
    ).transpose(0, 2, 1)
    gain_one_own = lax.dynamic_slice_in_dim(gain_one_grad, shard_start, shard_width, 0)
    gain_two_own = lax.dynamic_slice_in_dim(gain_two_grad, shard_start, shard_width, 0)
    summed = lax.psum(
        (gain_one_own, grad_qkv, grad_attn_out, gain_two_own, grad_ffn_in, grad_ffn_out),
        ("ctx", "seq"),
    )
    return (output, grad_tokens, summed[0], summed[1], summed[2], summed[3], summed[4], summed[5])


def solution(mesh):
    return jax.shard_map(
        local,
        mesh=mesh,
        in_specs=(
            P("seq", "wa", "ctx"),
            P("wa"),
            P(None, "wa", None),
            P("wa", None),
            P("wa"),
            P(None, "wa", None),
            P("wa", None),
            P("seq", "wa", "ctx"),
        ),
        out_specs=(
            P("seq", "wa", "ctx"),
            P("seq", "wa", "ctx"),
            P("wa"),
            P(None, "wa", None),
            P("wa", None),
            P("wa"),
            P(None, "wa", None),
            P("wa", None),
        ),
        check_vma=False,
    )
```

profile of v0, /device:TPU:0, one launch (start us, length us, event | category | flops | bytes accessed | tf_op | source)
XLA Modules:
  0.0 1963.5 jit_solution(11317879042997007579)
XLA Ops:
  21.8 36.9 %all-gather.6.cloned.1.call-done = bf16[4,768,1024]{2,1,0:T(8,128)(2,1)} async-done(((bf16[4,192,1024]{2,1,0:T(8,128)(2,1)}), bf16[4,768,1024]{2,1,0:T(8,128)(2,1)}) %all-gather.6.cloned.1.call-update) | async-done | bytes 6291472 | tf_op jit(solution)/shard_map/all_gather | solution.py:165
  85.9 110.0 %all-gather.8.cloned.1.call-done = bf16[4,3,4096,64]{2,3,1,0:T(8,128)(2,1)} async-done(((bf16[4,3,1024,64]{2,3,1,0:T(8,128)(2,1)}), bf16[4,3,4096,64]{2,3,1,0:T(8,128)(2,1)}) %all-gather.8.cloned.1.call-update) | async-done | bytes 6291472 | tf_op jit(solution)/shard_map/all_gather | solution.py:185
  195.8 188.9 %while.39 = (s32[]{:T(128)}, f32[4,3,1024]{2,1,0:T(4,128)S(1)}, f32[4,3,1024]{2,1,0:T(4,128)S(1)}, s32[8]{0:T(128)S(1)}, bf16[4,3,4096,64]{2,3,1,0:T(8,128)(2,1)...) while((s32[]{:T(128)}, f32[4,3,1024]{2,1,0:T(4,128)S(1)}, ...), condition=%wide.region_5.6_spmd.clone, body=%wide.region_2.5_spmd.clone.sunk | while | flops 836825088 | bytes 53330100 | solution.py:73
  197.1 12.5 bitcast_reduce_fusion.2
  209.6 10.5 fusion.226
  221.5 11.5 bitcast_reduce_fusion.2
  233.0 10.5 fusion.226
  244.9 11.5 bitcast_reduce_fusion.2
  256.4 10.6 fusion.226
  268.3 11.4 bitcast_reduce_fusion.2
  279.7 10.5 fusion.226
  291.6 11.3 bitcast_reduce_fusion.2
  303.0 10.5 fusion.226
  314.8 12.6 bitcast_reduce_fusion.2
  327.5 10.6 fusion.226
  339.4 11.4 bitcast_reduce_fusion.2
  350.8 10.6 fusion.226
  362.7 11.3 bitcast_reduce_fusion.2
  374.1 10.5 fusion.226
  384.8 92.7 %while.40 = (s32[]{:T(128)}, f32[4,3,1024,64]{2,3,1,0:T(8,128)}, s32[8]{0:T(128)S(1)}, bf16[4,3,4096,64]{2,3,1,0:T(8,128)(2,1)}, bf16[4,3,1024,64]{2,3,1,0:T(8,1...) while((s32[]{:T(128)}, f32[4,3,1024,64]{2,3,1,0:T(8,128)}, ...), condition=%wide.region_7.8_spmd.clone, body=%wide.region_6.7_spmd.clone.sunk | while | flops 1631059968 | bytes 9488056 | solution.py:93
  396.7 10.5 select_add_fusion.4
  408.4 10.5 select_add_fusion.4
  502.5 12.7 copy.52
  522.2 80.5 %all-reduce.12.cloned.1.call-done = bf16[4096,768]{1,0:T(8,128)(2,1)} async-done(((bf16[4096,768]{1,0:T(8,128)(2,1)}), bf16[4096,768]{1,0:T(8,128)(2,1)}) %all-reduce.12.cloned.1.call-update) | async-done | bytes 6291472 | tf_op jit(solution)/shard_map/psum | solution.py:194
  602.7 12.1 fusion.182
  629.5 12.5 fusion.104
  660.4 116.5 %all-reduce.14.cloned.1.call-done = bf16[4096,768]{1,0:T(8,128)(2,1)} async-done(((bf16[4096,768]{1,0:T(8,128)(2,1)}), bf16[4096,768]{1,0:T(8,128)(2,1)}) %all-reduce.14.cloned.1.call-update) | async-done | bytes 6291472 | tf_op jit(solution)/shard_map/psum | solution.py:225
  787.2 14.6 fusion.179
  811.2 471.1 %while.41 = (s32[]{:T(128)}, f32[4,3,1024,64]{2,3,1,0:T(8,128)}, f32[4,3,4096,64]{2,3,1,0:T(8,128)}, bf16[4,3,4096,64]{2,3,1,0:T(8,128)(2,1)}, s32[8]{0:T(128)S(...) while((s32[]{:T(128)}, f32[4,3,1024,64]{2,3,1,0:T(8,128)}, ...), condition=%wide.region_17.18_spmd.clone, body=%wide.region_16.17_spmd.clone.sunk | while | flops 4078436352 | bytes 137773328 | solution.py:133
  812.7 11.4 fusion.241
  824.1 11.5 fusion.242
  835.6 15.4 multiply_convert_fusion.7
  870.7 11.4 fusion.241
  882.1 11.5 fusion.242
  893.6 15.4 multiply_convert_fusion.7
  929.6 11.4 fusion.241
  941.0 11.5 fusion.242
  952.6 15.4 multiply_convert_fusion.7
  988.6 11.4 fusion.241
  1000.0 11.5 fusion.242
  1011.5 15.4 multiply_convert_fusion.7
  1047.5 11.4 fusion.241
  1059.0 11.4 fusion.242
  1070.4 15.4 multiply_convert_fusion.7
  1106.4 11.4 fusion.241
  1117.8 11.5 fusion.242
  1129.3 15.4 multiply_convert_fusion.7
  1165.4 11.4 fusion.241
  1176.8 11.4 fusion.242
  1188.3 15.4 multiply_convert_fusion.7
  1224.2 11.4 fusion.241
  1235.7 11.5 fusion.242
  1247.2 15.4 multiply_convert_fusion.7
  1295.2 10.6 negate_multiply_fusion
  1326.6 18.8 convert_bitcast_fusion.1
  1345.5 11.6 copy.64
  1361.3 40.9 %reduce-scatter.3.cloned.1.call-done = bf16[4,3,1024,64]{2,3,1,0:T(8,128)(2,1)} async-done(((bf16[4,3,4096,64]{2,3,1,0:T(8,128)(2,1)}), bf16[4,3,1024,64]{2,3,1,0:T(8,128)(2,1)}) %reduce-scatter.3.cloned.1.call-update) | async-done | bytes 1572880 | tf_op jit(solution)/shard_map/reduce_scatter | solution.py:247
  1407.2 108.7 %reduce-scatter.5.cloned.1.call-done = bf16[4,3,1024,64]{2,3,1,0:T(8,128)(2,1)} async-done(((bf16[4,3,4096,64]{2,3,1,0:T(8,128)(2,1)}), bf16[4,3,1024,64]{2,3,1,0:T(8,128)(2,1)}) %reduce-scatter.5.cloned.1.call-update) | async-done | bytes 1572880 | tf_op jit(solution)/shard_map/reduce_scatter | solution.py:250
  1545.6 11.8 fusion.100
  1557.4 15.9 fusion.102
  1593.4 172.3 %all-reduce.18.cloned.1.call-done = (bf16[4,768,1024]{2,0,1:T(4,128)(2,1)}, bf16[4096,768]{1,0:T(8,128)(2,1)}) async-done(((bf16[4,768,1024]{2,0,1:T(4,128)(2,1)}, bf16[4096,768]{1,0:T(8,128)(2,1)}), (bf16[4,768,1024]{2,0,1:T(4,128)(2,1)}, bf16[4096,768]{1,0:T(8,128)(2,1)})) %all-reduce.18.cloned.1.call-update) | async-done | bytes 12582928
  1781.1 13.4 fusion.44
  1805.6 22.8 %all-reduce.3 = (f32[192]{0:T(256)}, f32[192]{0:T(256)}) all-reduce(f32[192]{0:T(256)S(1)} %dynamic_slice.39, f32[192]{0:T(256)S(1)} %dynamic_slice.40), channel_id=1, replica_groups=mesh['ctx'=4,'seq'=2,'wa'=4] {'ctx','seq'}, use_global_device_ids=true, to_apply=%region_24.25 | all-reduce | flops 384 | bytes 3072 | tf_op jit(solution)/shard_map/psum | solution.py:275
  1828.4 120.8 %all-reduce.16.cloned.1.call-done = (f32[3,192,768]{2,1,0:T(8,128)}, f32[192,768]{1,0:T(8,128)}, f32[2,288,768]{2,1,0:T(8,128)}, f32[288,768]{1,0:T(8,128)}) async-done(((f32[3,192,768]{2,1,0:T(8,128)}, f32[192,768]{1,0:T(8,128)}, f32[2,288,768]{2,1,0:T(8,128)}, f32[288,768]{1,0:T(8,128)}), (f32[3,192,768]{2,1,0:T(8,128)}, f32[192,768]{1,0:T(8,128)}, f32[2,288,768]{2,1,0:T(8,128)}, ...) | async-done | bytes 5013520 | tf_op jit(solution)/shard_map/psum | solution.py:275
  (283 shorter events, 481.7 us)
Async XLA Ops:
  7.2 58.8 %copy-start = (bf16[3,192,768]{2,1,0:T(8,128)(2,1)S(1)}, bf16[3,192,768]{2,1,0:T(8,128)(2,1)}, u32[]{:S(2)}) copy-start(bf16[3,192,768]{2,1,0:T(8,128)(2,1)} %param.16) | copy-start | bytes 2654212
  7.2 51.5 %all-gather.6.cloned.1.call-start = ((), (), s32[]{:S(2)}) async-start(), calls=%async_computation.2 | async-start | bytes 7864320 | tf_op jit(solution)/shard_map/all_gather | solution.py:165
  7.9 187.9 %all-gather.8.cloned.1.call-start = ((), (), s32[]{:S(2)}) async-start(), calls=%async_computation.3 | async-start | bytes 7864320 | tf_op jit(solution)/shard_map/all_gather | solution.py:185
  20.6 45.4 %copy-start.27 = (f32[768]{0:T(1024)}, f32[768]{0:T(1024)S(1)}, u32[]{:S(2)}) copy-start(f32[768]{0:T(1024)S(1)} %convert_element_type.105) | copy-start | bytes 9220
  21.8 55.2 %copy-start.13 = (f32[1024,32]{0,1:T(8,128)}, f32[1024,32]{0,1:T(8,128)S(1)}, u32[]{:S(2)}) copy-start(f32[1024,32]{0,1:T(8,128)S(1)} %get-tuple-element.359) | copy-start | bytes 393220
  58.7 5.0 copy-start.3
  63.7 9.6 copy-start.23
  66.0 0.6 copy-start.31
  73.3 3.7 copy-start.8
  80.3 304.4 %all-gather.12.cloned.1.call-start = ((), (), s32[]{:S(2)}) async-start(), calls=%async_computation.9 | async-start | bytes 7864320 | tf_op jit(solution)/shard_map/all_gather | solution.py:186
  83.7 401.2 %all-gather.10.cloned.1.call-start = ((), (), s32[]{:S(2)}) async-start(), calls=%async_computation.5 | async-start | bytes 7864320 | tf_op jit(solution)/shard_map/all_gather | solution.py:166
  84.2 518.5 %all-reduce.12.cloned.1.call-start = ((), (), s32[]{:S(2)}) async-start(), calls=%async_computation.4 | async-start | bytes 12582912 | tf_op jit(solution)/shard_map/psum | solution.py:194
  477.4 2.3 copy-start.35
  484.2 0.7 copy-start.33
  484.2 292.7 %all-reduce.14.cloned.1.call-start = ((), (), s32[]{:S(2)}) async-start(), calls=%async_computation.6 | async-start | bytes 12582912 | tf_op jit(solution)/shard_map/psum | solution.py:225
  484.9 302.3 %copy-start.29 = (f32[768]{0:T(1024)}, f32[768]{0:T(1024)S(1)}, u32[]{:S(2)}) copy-start(f32[768]{0:T(1024)S(1)} %convert_element_type.112) | copy-start | bytes 9220
  502.5 12.7 copy-start.17
  614.8 172.3 %copy-start.19 = (f32[4096]{0:T(1024)}, f32[4096]{0:T(1024)S(1)}, u32[]{:S(2)}) copy-start(f32[4096]{0:T(1024)S(1)} %broadcast_multiply_fusion.5) | copy-start | bytes 49156
  614.9 6.2 copy-start.34
  614.9 14.5 slice-start.5
  621.1 166.1 %copy-start.21 = (f32[4096]{0:T(1024)}, f32[4096]{0:T(1024)S(1)}, u32[]{:S(2)}) copy-start(f32[4096]{0:T(1024)S(1)} %add_rsqrt_fusion) | copy-start | bytes 49156
  621.1 8.3 slice-start.6
  629.4 12.6 copy-start.2
  657.0 745.3 %reduce-scatter.3.cloned.1.call-start = ((), (), s32[]{:S(2)}) async-start(), calls=%async_computation.7 | async-start | bytes 7864320 | tf_op jit(solution)/shard_map/reduce_scatter | solution.py:247
  776.9 10.3 copy-start.5
  787.2 14.6 copy-start.6
  801.8 3.4 copy-start.9
  812.7 11.5 copy-start.1
  870.7 11.5 copy-start.1
  929.6 11.5 copy-start.1
  988.6 11.5 copy-start.1
  1047.5 11.5 copy-start.1
  1106.4 11.5 copy-start.1
  1165.4 11.5 copy-start.1
  1224.2 11.5 copy-start.1
  1291.1 224.7 %reduce-scatter.5.cloned.1.call-start = ((), (), s32[]{:S(2)}) async-start(), calls=%async_computation.8 | async-start | bytes 7864320 | tf_op jit(solution)/shard_map/reduce_scatter | solution.py:250
  1291.9 473.8 %all-reduce.18.cloned.1.call-start = ((), (), s32[]{:S(2)}) async-start(), calls=%async_computation.11 | async-start | bytes 25165824
  1319.7 7.0 copy-start.18
  1357.0 47.2 %copy-start.14 = (f32[1024,32]{0,1:T(8,128)S(1)}, f32[1024,32]{0,1:T(8,128)}, u32[]{:S(2)}) copy-start(f32[1024,32]{0,1:T(8,128)} %copy-done.13) | copy-start | bytes 393220
  1357.1 47.2 %copy-start.16 = (f32[1024,32]{0,1:T(8,128)S(1)}, f32[1024,32]{0,1:T(8,128)}, u32[]{:S(2)}) copy-start(f32[1024,32]{0,1:T(8,128)} %get-tuple-element.357) | copy-start | bytes 393220
  1402.3 2.4 copy-start.7
  1543.9 1.7 copy-start.10
  1543.9 1.7 copy-start.20
  1543.9 1.7 copy-start.22
  1543.9 1.7 copy-start.30
  1543.9 405.2 %all-reduce.16.cloned.1.call-start = ((), (), s32[]{:S(2)}) async-start(), calls=%async_computation.10 | async-start | bytes 10027008 | tf_op jit(solution)/shard_map/psum | solution.py:275
  1545.6 27.8 %slice-start.7 = ((s8[6291456]{0:T(1024)(128)(4,1)}), s8[4194304]{0:T(1024)(128)(4,1)S(1)}, s32[]{:S(2)}) async-start(s8[6291456]{0:T(1024)(128)(4,1)} %bitcast.294), calls=%async_computation.19 | async-start | bytes 8388608
  1545.6 30.1 %slice-start.3 = ((s8[6291456]{0:T(1024)(128)(4,1)}), s8[2097152]{0:T(1024)(128)(4,1)S(1)}, s32[]{:S(2)}) async-start(s8[6291456]{0:T(1024)(128)(4,1)} %bitcast.287), calls=%async_computation.15 | async-start | bytes 4194304
  1557.4 16.0 slice-start.8
  1557.4 16.0 copy-start.12
  1557.4 18.3 slice-start.4
  1573.4 2.3 slice-start.9
  1573.4 2.3 copy-start.24
  1573.4 2.3 copy-start.28
  1573.4 2.3 copy-start.32
  1573.4 2.3 slice-start.10
  1581.0 0.7 copy-start.25
  1581.0 0.7 copy-start.26
  1765.7 5.1 copy-start.4
  1765.7 15.4 slice-start
  1770.7 10.3 slice-start.1
  1770.7 10.3 slice-start.2
  1949.2 4.9 copy-start.11
  1949.2 6.1 copy-start.15
Sparse Core Ops, SparseCore 0:
  9.6 49.0 all-gather.5
  80.4 115.3 all-gather.7
  198.0 113.5 all-gather.11
  313.0 44.5 all-gather.9
  484.4 118.3 all-reduce.11
  657.1 119.7 all-reduce.13
  1291.3 110.9 reduce-scatter.2
  1404.6 111.2 reduce-scatter.4
  1544.1 221.5 all-reduce.17
  1770.1 179.0 all-reduce.15
where the time goes:
time: 1980 us; the launch traced here: 1960 us
  waiting for transfers between devices  789 us (40%)
  matrix products  740 us (37%)
  other arithmetic  236 us (12%)
  local copies, waits for them, and re-layouts  133 us (7%)
  blocking collectives  31.8 us (2%)
    dot_general x16, matrix products, scores_of(): jnp.einsum('shqe,shke->shqk', queries, keys_part, preferred_element_type=...  185 us
    unnamed x11, waiting for transfers between devices  174 us
    dot_general x8, matrix products, query_key_step(): jnp.einsum('shqe,shke->shqk', grad_out_low, values_part, preferred_elemen...  123 us
    psum x1, waiting for transfers between devices, local(): lax.psum((gain_one_own, grad_qkv, grad_attn_out, gain_two_own, grad_ffn_i...  121 us
    psum x1, waiting for transfers between devices, local(): lax.psum(jnp.einsum('tkf,kfd->td', grad_gate_up, ffn_in_weight, preferred...  116 us
    all_gather x1, waiting for transfers between devices, local(): lax.all_gather(keys_own, 'ctx', axis=2, tiled=True)  110 us
    reduce_scatter x1, waiting for transfers between devices, local(): lax.psum_scatter(grad_values_all.astype(jnp.bfloat16), 'ctx', scatter_dim...  109 us
    dot_general x8, matrix products, query_key_step(): jnp.einsum('shqk,shqe->shke', prob_rows.astype(jnp.bfloat16), grad_out_lo...  91.9 us
  transfers between devices with their start and end apart: 10, of which 8 were waited for; matrix products, arithmetic and copies ran while one was open for 25% of the time, Pallas kernels for 0%

commit v1 on v0

v1 whole, which is shorter than its diff:
```python
import functools
import math

import jax
import jax.numpy as jnp
from jax import lax
from jax.experimental import pallas as pl
from jax.experimental.pallas import tpu as pltpu
from jax.sharding import PartitionSpec as P

HD = 64
EPSILON = 1e-05
THETA_BASE = 160000.0
GROUPS = 3
LOG2E = math.log2(math.e)
F32 = jnp.float32
BF16 = jnp.bfloat16


def dot(a, b, contract_a, contract_b):
    return lax.dot_general(
        a, b, (((contract_a,), (contract_b,)), ((), ())), preferred_element_type=F32
    )


def rope_tables(positions, head_size):
    half_size = head_size // 2
    frequency = THETA_BASE ** (-jnp.arange(half_size, dtype=F32) * 2.0 / head_size)
    angles = frequency[:, None] * positions.astype(F32)[None, :]
    return (jnp.cos(angles), jnp.sin(angles))


def rotate(values, cosine_table, sine_table):
    half_size = values.shape[1] // 2
    first_half = values[:, :half_size]
    second_half = values[:, half_size:]
    return jnp.concatenate(
        [
            first_half * cosine_table - second_half * sine_table,
            second_half * cosine_table + first_half * sine_table,
        ],
        axis=1,
    )


def normalize(columns_in):
    center = columns_in - jnp.mean(columns_in, axis=0, keepdims=True)
    inverse = lax.rsqrt(jnp.mean(center * center, axis=0, keepdims=True) + EPSILON)
    return (center * inverse, inverse)


def norm_back(grad_hat, normed_hat, inverse):
    mean_grad = jnp.mean(grad_hat, axis=0, keepdims=True)
    mean_proj = jnp.mean(grad_hat * normed_hat, axis=0, keepdims=True)
    return inverse * (grad_hat - mean_grad - normed_hat * mean_proj)


def forward_kernel(q_ref, kv_ref, out_ref, lse_ref, acc_ref, max_ref, *, key_tile):
    queries = q_ref[0]
    blocks, length = kv_ref.shape[0], kv_ref.shape[4]
    acc_ref[...] = jnp.zeros_like(acc_ref)
    max_ref[...] = jnp.full_like(max_ref, -jnp.inf)

    def block_step(block, carry):
        for start in range(0, length, key_tile):
            keys = kv_ref[block, 0, 0, :, pl.ds(start, key_tile)]
            values = kv_ref[block, 1, 0, :, pl.ds(start, key_tile)]
            scores = dot(keys, queries, 0, 0)
            old_max = max_ref[...]
            new_max = jnp.maximum(old_max, jnp.max(scores, axis=0, keepdims=True))
            weights = jnp.exp2(scores - new_max).astype(BF16)
            values_ones = jnp.concatenate([values, jnp.ones((16, key_tile), BF16)], axis=0)
            acc_ref[...] = acc_ref[...] * jnp.exp2(old_max - new_max) + dot(
                values_ones, weights, 1, 0
            )
            max_ref[...] = new_max
        return carry

    lax.fori_loop(0, blocks, block_step, 0)
    total = acc_ref[HD : HD + 1, :]
    out_ref[0] = acc_ref[:HD, :] / total
    lse_ref[0] = max_ref[...] + jnp.log2(total)


def attend(queries, kv_all):
    heads, head_size, length = queries.shape
    blocks, key_length = kv_all.shape[0], kv_all.shape[4]
    pairs = heads * length * blocks * key_length
    return pl.pallas_call(
        functools.partial(forward_kernel, key_tile=math.gcd(key_length, 512)),
        grid=(heads,),
        in_specs=[
            pl.BlockSpec((1, head_size, length), lambda h: (h, 0, 0)),
            pl.BlockSpec((blocks, 2, 1, head_size, key_length), lambda h: (0, 0, h, 0, 0)),
        ],
        out_specs=[
            pl.BlockSpec((1, head_size, length), lambda h: (h, 0, 0)),
            pl.BlockSpec((1, 1, length), lambda h: (h, 0, 0)),
        ],
        out_shape=[
            jax.ShapeDtypeStruct((heads, head_size, length), F32),
            jax.ShapeDtypeStruct((heads, 1, length), F32),
        ],
        scratch_shapes=[pltpu.VMEM((head_size + 16, length), F32), pltpu.VMEM((1, length), F32)],
        compiler_params=pltpu.CompilerParams(vmem_limit_bytes=48 * 1024 * 1024),
        cost_estimate=pl.CostEstimate(
            flops=16 * pairs * head_size, bytes_accessed=4 * kv_all.size, transcendentals=pairs
        ),
    )(queries, kv_all)


def split_rows(row, count):
    high = row.astype(BF16).astype(F32)
    middle = (row - high).astype(BF16).astype(F32)
    least = row - high - middle
    index = lax.broadcasted_iota(jnp.int32, (count, row.shape[1]), 0)
    stacked = jnp.where(
        index == 0, high, jnp.where(index == 1, middle, jnp.where(index == 2, least, 0.0))
    )
    return stacked.astype(BF16)


def backward_kernel(q_ref, kv_ref, go_ref, out_ref, lse_ref, gq_ref, gkv_ref, *, key_tile):
    queries = q_ref[0]
    grad_out = go_ref[0]
    blocks, length = kv_ref.shape[0], kv_ref.shape[4]
    grad_dot = jnp.sum(grad_out.astype(F32) * out_ref[0], axis=0, keepdims=True)
    queries_more = jnp.concatenate([queries, split_rows(lse_ref[0], 16)], axis=0)
    grad_more = jnp.concatenate([grad_out, split_rows(grad_dot, 16)], axis=0)
    index = lax.broadcasted_iota(jnp.int32, (16, key_tile), 0)
    minus = jnp.where(index < 3, -1.0, 0.0).astype(BF16)
    gq_ref[...] = jnp.zeros_like(gq_ref)

    def block_step(block, carry):
        for start in range(0, length, key_tile):
            keys = kv_ref[block, 0, 0, :, pl.ds(start, key_tile)]
            values = kv_ref[block, 1, 0, :, pl.ds(start, key_tile)]
            probs = jnp.exp2(dot(jnp.concatenate([keys, minus], axis=0), queries_more, 0, 0))
            grad_probs = dot(jnp.concatenate([values, minus], axis=0), grad_more, 0, 0)
            grad_scores = (probs * grad_probs).astype(BF16)
            gq_ref[0] += dot(keys, grad_scores, 1, 0)
            grad_keys = dot(queries, grad_scores, 1, 1) * (1.0 / LOG2E)
            grad_values = dot(grad_out, probs.astype(BF16), 1, 1)
            gkv_ref[block, 0, 0, :, pl.ds(start, key_tile)] = grad_keys.astype(BF16)
            gkv_ref[block, 1, 0, :, pl.ds(start, key_tile)] = grad_values.astype(BF16)
        return carry

    lax.fori_loop(0, blocks, block_step, 0)


def attend_back(queries, kv_all, grad_out, out, lse):
    heads, head_size, length = queries.shape
    blocks, key_length = kv_all.shape[0], kv_all.shape[4]
    pairs = heads * length * blocks * key_length
    per_head = pl.BlockSpec((1, head_size, length), lambda h: (h, 0, 0))
    per_kv = pl.BlockSpec((blocks, 2, 1, head_size, key_length), lambda h: (0, 0, h, 0, 0))
    return pl.pallas_call(
        functools.partial(backward_kernel, key_tile=math.gcd(key_length, 512)),
        grid=(heads,),
        in_specs=[
            per_head,
            per_kv,
            per_head,
            per_head,
            pl.BlockSpec((1, 1, length), lambda h: (h, 0, 0)),
        ],
        out_specs=[per_head, per_kv],
        out_shape=[
            jax.ShapeDtypeStruct((heads, head_size, length), F32),
            jax.ShapeDtypeStruct(kv_all.shape, BF16),
        ],
        compiler_params=pltpu.CompilerParams(vmem_limit_bytes=48 * 1024 * 1024),
        cost_estimate=pl.CostEstimate(
            flops=40 * pairs * head_size, bytes_accessed=8 * kv_all.size, transcendentals=pairs
        ),
    )(queries, kv_all, grad_out, out, lse)


def local(
    tokens,
    first_gain,
    qkv_weight,
    attn_out_weight,
    second_gain,
    ffn_in_weight,
    ffn_out_weight,
    cotangent,
):
    wa_size = lax.axis_size("wa")
    length = tokens.shape[2]
    width = qkv_weight.shape[2]
    shard = qkv_weight.shape[1]
    hidden_shard = ffn_in_weight.shape[1]
    heads = width // HD
    assert tokens.shape[0] == wa_size
    per_group = heads // GROUPS
    score_scale = 1.0 / math.sqrt(HD)

    x_low = lax.all_to_all(tokens, "wa", 0, 1, tiled=True)[0]
    qkv_all = lax.all_gather(qkv_weight, "wa", axis=0)
    gains = lax.all_gather(jnp.stack([first_gain, second_gain]), "wa", axis=0)
    gains = gains.transpose(1, 0, 2).reshape(2, width, 1).astype(F32)
    gain_one, gain_two = gains[0], gains[1]
    cot = lax.all_to_all(cotangent, "wa", 0, 1, tiled=True)[0]
    attn_mat = lax.all_gather(attn_out_weight, "wa", axis=0).reshape(width, width)
    ffn_in_mat = lax.all_gather(ffn_in_weight, "wa", axis=0).reshape(-1, width)
    ffn_out_mat = lax.all_gather(ffn_out_weight, "wa", axis=0).reshape(-1, width)
    qkv_mat = qkv_all.reshape(-1, width)

    x = x_low.astype(F32)
    hat_one, inv_one = normalize(x)
    normed_one = (hat_one * gain_one).astype(BF16)
    projected = dot(qkv_mat, normed_one, 1, 0).reshape(wa_size, 3, shard, length)
    positions = lax.axis_index("ctx") * length + jnp.arange(length, dtype=jnp.int32)
    cosine_table, sine_table = rope_tables(positions, HD)

    def by_head(index):
        return projected[:, index].reshape(heads, HD, length)

    queries = rotate(
        by_head(0), cosine_table * (score_scale * LOG2E), sine_table * (score_scale * LOG2E)
    ).astype(BF16)
    keys_own = rotate(by_head(1), cosine_table, sine_table).astype(BF16)
    values_own = by_head(2).astype(BF16)

    parts = []
    for group in range(GROUPS):
        rows = slice(group * per_group, (group + 1) * per_group)
        kv_all = lax.all_gather(jnp.stack([keys_own[rows], values_own[rows]]), "ctx", axis=0)
        parts.append((rows, kv_all))
    results = [attend(queries[rows], kv_all) for rows, kv_all in parts]
    attended_low = jnp.concatenate([r[0].astype(BF16) for r in results], axis=0).reshape(
        width, length
    )
    middle = x + dot(attn_mat, attended_low, 0, 0)
    hat_two, inv_two = normalize(middle)
    normed_two = (hat_two * gain_two).astype(BF16)
    gate_up = dot(ffn_in_mat, normed_two, 1, 0).reshape(wa_size, 2, hidden_shard, length)
    gate, up = gate_up[:, 0], gate_up[:, 1]
    cdf = 0.5 * (1.0 + lax.erf(gate * math.sqrt(0.5)))
    gelu = gate * cdf
    hidden = (gelu * up).astype(BF16).reshape(-1, length)
    output_all = (middle + dot(ffn_out_mat, hidden, 0, 0)).astype(BF16)
    output = lax.all_to_all(output_all[None], "wa", 1, 0, tiled=True)

    grad_ffn_out = dot(hidden, cot, 1, 1)
    grad_hidden = dot(ffn_out_mat, cot, 1, 0).reshape(gate.shape)
    slope = cdf + gate * (jnp.exp(-0.5 * gate * gate) * (1.0 / math.sqrt(2.0 * math.pi)))
    grad_gate_up = (
        jnp.stack([grad_hidden * up * slope, grad_hidden * gelu], axis=1)
        .astype(BF16)
        .reshape(-1, length)
    )
    grad_ffn_in = dot(grad_gate_up, normed_two, 1, 1)
    grad_normed_two = dot(ffn_in_mat, grad_gate_up, 0, 0)
    gain_two_grad = jnp.sum(grad_normed_two * hat_two, axis=1)
    grad_middle = cot.astype(F32) + norm_back(grad_normed_two * gain_two, hat_two, inv_two)
    grad_middle_low = grad_middle.astype(BF16)
    grad_attn_out = dot(attended_low, grad_middle_low, 1, 1)
    grad_attended = dot(attn_mat, grad_middle_low, 1, 0).astype(BF16).reshape(heads, HD, length)

    def sum_weights(grads):
        own = lax.psum_scatter(grads.astype(BF16), "wa", scatter_dimension=0)
        return lax.psum(own, ("ctx", "seq")).astype(F32)

    early = sum_weights(
        jnp.concatenate(
            [
                grad_ffn_in.astype(BF16).reshape(wa_size, -1, width),
                grad_ffn_out.astype(BF16).reshape(wa_size, -1, width),
                grad_attn_out.astype(BF16).reshape(wa_size, -1, width),
            ],
            axis=1,
        )
    )
    grad_ffn_in_own = early[: 2 * hidden_shard].reshape(2, hidden_shard, width)
    grad_ffn_out_own = early[2 * hidden_shard : 3 * hidden_shard]
    grad_attn_out_own = early[3 * hidden_shard :]

    grad_queries, grad_kv = [], []
    for (rows, kv_all), (out, lse) in zip(parts, results):
        grad_q, grad_kv_all = attend_back(queries[rows], kv_all, grad_attended[rows], out, lse)
        grad_queries.append(grad_q)
        grad_kv.append(lax.psum_scatter(grad_kv_all, "ctx", scatter_dimension=0))
    grad_q = jnp.concatenate(grad_queries, axis=0)
    grad_k = jnp.concatenate([g[0] for g in grad_kv], axis=0).astype(F32)
    grad_v = jnp.concatenate([g[1] for g in grad_kv], axis=0)
    grad_q = rotate(grad_q, cosine_table * score_scale, -sine_table * score_scale).astype(BF16)
    grad_k = rotate(grad_k, cosine_table, -sine_table).astype(BF16)
    grad_projected = jnp.stack(
        [g.reshape(wa_size, shard, length) for g in (grad_q, grad_k, grad_v)], axis=1
    ).reshape(-1, length)
    grad_normed_one = dot(qkv_mat, grad_projected, 0, 0)
    gain_one_grad = jnp.sum(grad_normed_one * hat_one, axis=1)
    grad_x = grad_middle + norm_back(grad_normed_one * gain_one, hat_one, inv_one)
    grad_tokens = lax.all_to_all(grad_x.astype(BF16)[None], "wa", 1, 0, tiled=True).astype(F32)
    grad_qkv = dot(grad_projected, normed_one, 1, 1)
    grad_qkv_own = sum_weights(grad_qkv.reshape(wa_size, -1, width)).reshape(3, shard, width)
    gain_sums = lax.psum(jnp.stack([gain_one_grad, gain_two_grad]), ("ctx", "seq", "wa"))
    gain_own = lax.dynamic_slice_in_dim(gain_sums, lax.axis_index("wa") * shard, shard, 1)
    return (
        output,
        grad_tokens,
        gain_own[0],
        grad_qkv_own,
        grad_attn_out_own,
        gain_own[1],
        grad_ffn_in_own,
        grad_ffn_out_own,
    )


def solution(mesh):
    return jax.shard_map(
        local,
        mesh=mesh,
        in_specs=(
            P("seq", "wa", "ctx"),
            P("wa"),
            P(None, "wa", None),
            P("wa", None),
            P("wa"),
            P(None, "wa", None),
            P("wa", None),
            P("seq", "wa", "ctx"),
        ),
        out_specs=(
            P("seq", "wa", "ctx"),
            P("seq", "wa", "ctx"),
            P("wa"),
            P(None, "wa", None),
            P("wa", None),
            P("wa"),
            P(None, "wa", None),
            P("wa", None),
        ),
        check_vma=False,
    )
```

time: 1980 us -> 959 us (0.48)
  matrix products: 740 us -> 66.6 us
  waiting for transfers between devices: 789 us -> 392 us
  Pallas kernels: 0 us -> 238 us
  other arithmetic: 236 us -> 52.4 us
  blocking collectives: 31.8 us -> 81.4 us
  local copies, waits for them, and re-layouts: 133 us -> 88 us
    dot_general x68 -> x12, matrix products: 740 us -> 66.6 us  [dot(): lax.dot_general(a, b, (((contract_a,), (contract_b,)), ((), ())), preferr...]
    psum x3 -> x1, waiting for transfers between devices: 318 us -> 24.8 us  [sum_weights(): return lax.psum(own, ('ctx', 'seq')).astype(F32)]
    pallas_call x0 -> x6, Pallas kernels: none -> 238 us  [the longest x3 145 us: attend_back(): pl.pallas_call(functools.partial(backward_kernel, key_tile=math.gcd(key_l...]
    unnamed x11 -> x13, waiting for transfers between devices: 174 us -> 2.58 us
    reduce_sum x14 -> x3, other arithmetic: 129 us -> 1.11 us  [the longest x2 0.85 us: normalize(): jnp.mean(center * center, axis=0, keepdims=True) + EPSILON]
    all_gather x4 -> x7, waiting for transfers between devices: 147 us -> 181 us  [the longest x3 166 us: local(): lax.all_gather(jnp.stack([keys_own[rows], values_own[rows]]), 'ctx', axis=0)]
    reduce_scatter x2 -> x5, waiting for transfers between devices: 150 us -> 183 us  [the longest x3 108 us: local(): grad_kv.append(lax.psum_scatter(grad_kv_all, 'ctx', scatter_dimension=0))]
    all_gather x0 -> x1, blocking collectives: none -> 31.3 us  [local(): gains = lax.all_gather(jnp.stack([first_gain, second_gain]), 'wa', axis=0)]
  transfers between devices with their start and end apart: 10 -> 17, of which waited for: 8 -> 11; matrix products, arithmetic and copies ran while one was open for 25% -> 14% of each run, Pallas kernels for 0% -> 20%
where the time goes in v1:
time: 959 us; the launch traced here: 951 us
  waiting for transfers between devices  392 us (41%)
  Pallas kernels  238 us (25%)
  local copies, waits for them, and re-layouts  88 us (9%)
  blocking collectives  81.4 us (8%)
  matrix products  66.6 us (7%)
  other arithmetic  52.4 us (5%)
  starting transfers between devices  18.1 us (2%)
  between operations  15 us (2%)
    all_gather x3, waiting for transfers between devices, local(): lax.all_gather(jnp.stack([keys_own[rows], values_own[rows]]), 'ctx', axis=0)  166 us
    pallas_call x3, Pallas kernels, attend_back(): pl.pallas_call(functools.partial(backward_kernel, key_tile=math.gcd(key_l...  145 us
    reduce_scatter x3, waiting for transfers between devices, local(): grad_kv.append(lax.psum_scatter(grad_kv_all, 'ctx', scatter_dimension=0))  108 us
    pallas_call x3, Pallas kernels, attend(): pl.pallas_call(functools.partial(forward_kernel, key_tile=math.gcd(key_le...  92.4 us
    reduce_scatter x2, waiting for transfers between devices, sum_weights(): own = lax.psum_scatter(grads.astype(BF16), 'wa', scatter_dimension=0)  75.2 us
    dot_general x12, matrix products, dot(): lax.dot_general(a, b, (((contract_a,), (contract_b,)), ((), ())), preferr...  66.6 us
    psum x1, blocking collectives, local(): lax.psum(jnp.stack([gain_one_grad, gain_two_grad]), ('ctx', 'seq', 'wa'))  50.1 us
    unnamed x126, local copies, waits for them, and re-layouts  44 us
  transfers between devices with their start and end apart: 17, of which 11 were waited for; matrix products, arithmetic and copies ran while one was open for 14% of the time, Pallas kernels for 20%

profile of v1, /device:TPU:0, one launch (start us, length us, event | category | flops | bytes accessed | tf_op | source)
XLA Modules:
  0.0 951.0 jit_solution(8189390048998652204)
XLA Ops:
  7.9 4.2 all-to-all-start
  12.2 31.3 %all-gather.8 = bf16[4,2,192]{2,1,0:T(2,128)(2,1)S(1)} all-gather(bf16[1,2,192]{2,1,0:T(2,128)(2,1)S(1)} %maximum_bitcast_fusion), channel_id=2, replica_groups=mesh['ctx'=4,'seq'=2,'wa'=4] {'wa'}, dimensions={0}, use_global_device_ids=true | all-gather | bytes 3840 | tf_op jit(solution)/shard_map/all_gather | solution.py:201
  47.4 5.5 all-gather.17.cloned.1.call-done
  52.8 8.4 convolution_bitcast_fusion.1
  61.2 9.6 %copy.48 = f32[2304,1024]{1,0:T(8,128)} copy(f32[2304,1024]{0,1:T(8,128)} %convolution_bitcast_fusion.1) | data formatting | bytes 18874368 | tf_op jit(solution)/shard_map/dot_general | solution.py:21
  70.8 2.1 slice.294
  72.9 3.4 fusion.55
  80.2 2.3 pad_maximum_fusion.8
  82.6 2.3 pad_maximum_fusion.6
  86.0 4.4 all-to-all-start.2
  92.8 69.4 %all-gather.21.cloned.1.call-done = bf16[8,4,64,1024]{3,2,1,0:T(8,128)(2,1)} async-done(((bf16[2,4,64,1024]{3,2,1,0:T(8,128)(2,1)}), bf16[8,4,64,1024]{3,2,1,0:T(8,128)(2,1)}) %all-gather.21.cloned.1.call-update) | async-done | bytes 4194320 | tf_op jit(solution)/shard_map/all_gather | solution.py:229
  162.1 2.2 copy-done.10
  164.3 30.9 %shard_map.144 = (f32[4,64,1024]{2,1,0:T(8,128)S(1)}, f32[4,1,1024]{2,1,0:T(1,128)S(1)}) custom-call(bf16[4,64,1024]{2,1,0:T(8,128)(2,1)S(1)} %get-tuple-element.65.q_ref, bf16[4,2,4,64,1024]{4,3,2,1,0:T(8,128)(2,1)S(1)} %bitcast.233), custom_call_target="tpu_custom_call" | custom-call | flops 17179869184 | bytes 8388608 | tf_op jit(solution)/shard_map/pallas_call | solution.py:89
  195.3 48.5 %all-gather.23.cloned.1.call-done = bf16[8,4,64,1024]{3,2,1,0:T(8,128)(2,1)} async-done(((bf16[2,4,64,1024]{3,2,1,0:T(8,128)(2,1)}), bf16[8,4,64,1024]{3,2,1,0:T(8,128)(2,1)}) %all-gather.23.cloned.1.call-update) | async-done | bytes 4194320 | tf_op jit(solution)/shard_map/all_gather | solution.py:229
  243.7 2.2 copy-done.12
  245.9 30.7 %shard_map.145 = (f32[4,64,1024]{2,1,0:T(8,128)S(1)}, f32[4,1,1024]{2,1,0:T(1,128)S(1)}) custom-call(bf16[4,64,1024]{2,1,0:T(8,128)(2,1)S(1)} %get-tuple-element.64.q_ref, bf16[4,2,4,64,1024]{4,3,2,1,0:T(8,128)(2,1)S(1)} %bitcast.237), custom_call_target="tpu_custom_call" | custom-call | flops 17179869184 | bytes 8388608 | tf_op jit(solution)/shard_map/pallas_call | solution.py:89
  276.7 47.7 %all-gather.19.cloned.1.call-done = bf16[8,4,64,1024]{3,2,1,0:T(8,128)(2,1)} async-done(((bf16[2,4,64,1024]{3,2,1,0:T(8,128)(2,1)}), bf16[8,4,64,1024]{3,2,1,0:T(8,128)(2,1)}) %all-gather.19.cloned.1.call-update) | async-done | bytes 4194320 | tf_op jit(solution)/shard_map/all_gather | solution.py:229
  325.4 2.2 copy-done.11
  327.6 30.7 %shard_map.143 = (f32[4,64,1024]{2,1,0:T(8,128)S(1)}, f32[4,1,1024]{2,1,0:T(1,128)S(1)}) custom-call(bf16[4,64,1024]{2,1,0:T(8,128)(2,1)S(1)} %copy-done.4, bf16[4,2,4,64,1024]{4,3,2,1,0:T(8,128)(2,1)S(1)} %bitcast.235), custom_call_target="tpu_custom_call" | custom-call | flops 17179869184 | bytes 8388608 | tf_op jit(solution)/shard_map/pallas_call | solution.py:89
  359.9 3.8 fusion.58
  363.7 1.6 copy-done.15
  365.7 8.3 all-gather.27.cloned.1.call-done
  374.0 10.8 %convolution_bitcast_fusion = f32[2304,1024]{0,1:T(8,128)} fusion(bf16[2304,768]{1,0:T(8,128)(2,1)} %bitcast.279, f32[768,1024]{1,0:T(8,128)} %copy-done.15, f32[768]{0:T(1024)S(1)} %mul.384, f32[1024]{0:T(1024)S(1)} %add_rsqrt_fusion, f32[1024]{0:T(1024)S(1)} %broadcast_multiply_fusion.5), kind=kOutput, calls=%fused_computation.3 | convolution fusion | flops 3627024384 | bytes 16133120 | tf_op jit(solution)/shard_map/dot_general | solution.py:21
  384.8 9.6 %copy.49 = f32[2304,1024]{1,0:T(8,128)} copy(f32[2304,1024]{0,1:T(8,128)} %convolution_bitcast_fusion) | data formatting | bytes 18874368 | tf_op jit(solution)/shard_map/dot_general | solution.py:21
  394.4 2.0 all-gather.29.cloned.1.call-done
  396.4 7.7 fusion.5
  404.1 5.5 fusion.15
  409.6 2.5 multiply_add_fusion
  412.2 1.4 fusion.37
  415.0 48.4 %shard_map.148 = (f32[4,64,1024]{2,1,0:T(8,128)S(1)}, bf16[4,2,4,64,1024]{4,3,2,1,0:T(8,128)(2,1)}) custom-call(bf16[4,64,1024]{2,1,0:T(8,128)(2,1)S(1)} %copy-done.7, bf16[4,2,4,64,1024]{4,3,2,1,0:T(8,128)(2,1)} %bitcast.236, bf16[4,64,1024]{2,1,0:T(8,128)(2,1)S(1)} %bitcast.231, f32[4,64,1024]{2,1,0:T(8,128)S(1)} %get-tuple-element.22.out_ref, ...), custom_call_target="tpu_custom_call" | custom-call | flops 42949672960 | bytes 16777216 | tf_op jit(solution)/shard_map/pallas_call | solution.py:157
  466.6 48.6 %shard_map.146 = (f32[4,64,1024]{2,1,0:T(8,128)S(1)}, bf16[4,2,4,64,1024]{4,3,2,1,0:T(8,128)(2,1)}) custom-call(bf16[4,64,1024]{2,1,0:T(8,128)(2,1)S(1)} %copy-done.5, bf16[4,2,4,64,1024]{4,3,2,1,0:T(8,128)(2,1)} %bitcast.234, bf16[4,64,1024]{2,1,0:T(8,128)(2,1)S(1)} %bitcast.230, f32[4,64,1024]{2,1,0:T(8,128)S(1)} %get-tuple-element.20.out_ref, ...), custom_call_target="tpu_custom_call" | custom-call | flops 42949672960 | bytes 16777216 | tf_op jit(solution)/shard_map/pallas_call | solution.py:157
  517.3 48.4 %shard_map.147 = (f32[4,64,1024]{2,1,0:T(8,128)S(1)}, bf16[4,2,4,64,1024]{4,3,2,1,0:T(8,128)(2,1)}) custom-call(bf16[4,64,1024]{2,1,0:T(8,128)(2,1)S(1)} %copy-done.3, bf16[4,2,4,64,1024]{4,3,2,1,0:T(8,128)(2,1)} %bitcast.232, bf16[4,64,1024]{2,1,0:T(8,128)(2,1)S(1)} %bitcast.229, f32[4,64,1024]{2,1,0:T(8,128)S(1)} %get-tuple-element.21.out_ref, ...), custom_call_target="tpu_custom_call" | custom-call | flops 42949672960 | bytes 16777216 | tf_op jit(solution)/shard_map/pallas_call | solution.py:157
  565.8 2.9 maximum_convert_fusion
  570.7 1.4 convolution_convert_fusion.4
  572.2 1.5 slice-done.2
  573.7 1.4 fusion.7
  575.1 3.6 convolution_convert_fusion.1
  578.8 4.4 convolution_convert_fusion
  583.2 3.4 pad_maximum_fusion
  591.3 29.8 %reduce-scatter.6.cloned.1.call-done = bf16[1,2,4,64,1024]{4,3,2,1,0:T(8,128)(2,1)} async-done(((bf16[4,2,4,64,1024]{4,3,2,1,0:T(8,128)(2,1)}), bf16[1,2,4,64,1024]{4,3,2,1,0:T(8,128)(2,1)}) %reduce-scatter.6.cloned.1.call-update) | async-done | bytes 1048592 | tf_op jit(solution)/shard_map/reduce_scatter | solution.py:284
  622.4 78.1 %reduce-scatter.8.cloned.1.call-done = bf16[1,2,4,64,1024]{4,3,2,1,0:T(8,128)(2,1)} async-done(((bf16[4,2,4,64,1024]{4,3,2,1,0:T(8,128)(2,1)}), bf16[1,2,4,64,1024]{4,3,2,1,0:T(8,128)(2,1)}) %reduce-scatter.8.cloned.1.call-update) | async-done | bytes 1048592 | tf_op jit(solution)/shard_map/reduce_scatter | solution.py:284
  702.1 2.9 subtract_convert_fusion
  708.2 5.4 convolution_convert_fusion.2
  714.3 1.6 copy-done.18
  715.9 6.3 fusion.34
  722.3 2.4 copy.78
  725.2 11.2 %reduce.10 = bf16[768,1024]{1,0:T(8,128)(2,1)} reduce(bf16[768,1,1024]{2,1,0:T(2,128)(2,1)S(1)} %bitcast.245, bf16[]{:T(256)} %broadcast.270), dimensions={1}, to_apply=%bitcast.228.reduce_sub_computation | reduce | bytes 3145730
  736.4 4.1 reshape.474
  740.5 4.6 all-to-all-start.1
  745.2 31.8 %reduce-scatter.14.cloned.1.call-done = bf16[1,1056,768]{2,1,0:T(8,128)(2,1)} async-done(((bf16[4,1056,768]{2,1,0:T(8,128)(2,1)}), bf16[1,1056,768]{2,1,0:T(8,128)(2,1)}) %reduce-scatter.14.cloned.1.call-update) | async-done | bytes 1622032 | tf_op jit(solution)/shard_map/reduce_scatter | solution.py:263
  777.0 43.4 %reduce-scatter.12.cloned.1.call-done = bf16[1,576,768]{2,1,0:T(8,128)(2,1)} async-done(((bf16[4,576,768]{2,1,0:T(8,128)(2,1)}), bf16[1,576,768]{2,1,0:T(8,128)(2,1)}) %reduce-scatter.12.cloned.1.call-update) | async-done | bytes 884752 | tf_op jit(solution)/shard_map/reduce_scatter | solution.py:263
  820.4 8.0 fusion.16
  829.5 2.4 copy.77
  831.9 11.2 %reduce.11 = bf16[768,1024]{1,0:T(8,128)(2,1)} reduce(bf16[768,1,1024]{2,1,0:T(2,128)(2,1)S(1)} %bitcast.246, bf16[]{:T(256)} %broadcast.270), dimensions={1}, to_apply=%bitcast.227.reduce_sub_computation | reduce | bytes 3145730
  843.2 4.1 reshape.476
  847.3 4.4 all-to-all-start.3
  851.7 3.1 reshape.475
  854.7 1.7 copy.65
  856.5 50.1 %psum.21 = f32[2,768]{1,0:T(2,128)S(1)} all-reduce(f32[2,768]{1,0:T(2,128)S(1)} %pad_maximum_fusion.11), channel_id=1, replica_groups=mesh['ctx'=4,'seq'=2,'wa'=4] {'ctx','seq','wa'}, use_global_device_ids=true, to_apply=%region_13.0 | all-reduce | flops 1536 | bytes 12288 | tf_op jit(solution)/shard_map/psum | solution.py:299
  907.2 3.1 reshape.477
  910.4 2.4 copy.66
  912.8 24.8 %all-reduce.3.cloned.1.call-done = (bf16[3,192,768]{2,1,0:T(8,128)(2,1)}, bf16[1056,768]{1,0:T(8,128)(2,1)}) async-done(((bf16[3,192,768]{2,1,0:T(8,128)(2,1)}, bf16[1056,768]{1,0:T(8,128)(2,1)}), (bf16[3,192,768]{2,1,0:T(8,128)(2,1)}, bf16[1056,768]{1,0:T(8,128)(2,1)})) %all-reduce.3.cloned.1.call-update) | async-done | bytes 2506768 | tf_op jit(solution)/shard_map/psum | solution.py:264
  937.6 2.0 slice.211
  939.5 2.0 slice.213
  (197 shorter events, 39.9 us)
Async XLA Ops:
  7.2 5.0 copy-start.53
  7.2 5.0 copy-start.54
  7.2 45.6 %all-gather.17.cloned.1.call-start = ((), (), s32[]{:S(2)}) async-start(), calls=%async_computation.14 | async-start | bytes 4423680 | tf_op jit(solution)/shard_map/all_gather | solution.py:200
  7.9 37.6 %all-to-all-start = ((bf16[4,192,1024]{2,1,0:T(8,128)(2,1)}), bf16[4,192,1024]{2,1,0:T(8,128)(2,1)S(1)}, u32[]{:S(2)}, u32[]{:S(2)}) async-start(bf16[4,192,1024]{2,1,0:T(8,128)(2,1)} %param.8), calls=%async_computation | async-start | bytes 3145728 | tf_op jit(solution)/shard_map/all_to_all | solution.py:199
  12.2 150.0 %all-gather.21.cloned.1.call-start = ((), (), s32[]{:S(2)}) async-start(), calls=%async_computation.16 | async-start | bytes 5242880 | tf_op jit(solution)/shard_map/all_gather | solution.py:229
  45.5 32.0 %copy-start.32 = (f32[32,1024]{1,0:T(8,128)}, f32[32,1024]{1,0:T(8,128)S(1)}, u32[]{:S(2)}) copy-start(f32[32,1024]{1,0:T(8,128)S(1)} %get-tuple-element.81) | copy-start | bytes 393220
  45.5 1.9 copy-start.13
  47.3 13.8 %copy-start.29 = (bf16[4,192,1024]{2,1,0:T(8,128)(2,1)}, bf16[4,192,1024]{2,1,0:T(8,128)(2,1)S(1)}, u32[]{:S(2)}) copy-start(bf16[4,192,1024]{2,1,0:T(8,128)(2,1)S(1)} %fusion.21) | copy-start | bytes 4718596
  80.2 163.6 %all-gather.23.cloned.1.call-start = ((), (), s32[]{:S(2)}) async-start(), calls=%async_computation.17 | async-start | bytes 5242880 | tf_op jit(solution)/shard_map/all_gather | solution.py:229
  82.5 241.8 %all-gather.19.cloned.1.call-start = ((), (), s32[]{:S(2)}) async-start(), calls=%async_computation.15 | async-start | bytes 5242880 | tf_op jit(solution)/shard_map/all_gather | solution.py:229
  84.9 275.0 %all-gather.25.cloned.1.call-start = ((), (), s32[]{:S(2)}) async-start(), calls=%async_computation.18 | async-start | bytes 1474560 | tf_op jit(solution)/shard_map/all_gather | solution.py:205
  85.5 288.6 %all-gather.27.cloned.1.call-start = ((), (), s32[]{:S(2)}) async-start(), calls=%async_computation.19 | async-start | bytes 4423680 | tf_op jit(solution)/shard_map/all_gather | solution.py:206
  86.0 308.3 %all-to-all-start.2 = ((bf16[4,192,1024]{2,1,0:T(8,128)(2,1)}), bf16[4,192,1024]{2,1,0:T(8,128)(2,1)}, u32[]{:S(2)}, u32[]{:S(2)}) async-start(bf16[4,192,1024]{2,1,0:T(8,128)(2,1)} %param.15), calls=%async_computation.2 | async-start | bytes 3145728 | tf_op jit(solution)/shard_map/all_to_all | solution.py:204
  90.5 305.9 %all-gather.29.cloned.1.call-start = ((), (), s32[]{:S(2)}) async-start(), calls=%async_computation.20 | async-start | bytes 2211840 | tf_op jit(solution)/shard_map/all_gather | solution.py:207
  91.2 498.7 %reduce-scatter.10.cloned.1.call-start = ((), (), s32[]{:S(2)}) async-start(), calls=%async_computation.11 | async-start | bytes 5242880 | tf_op jit(solution)/shard_map/reduce_scatter | solution.py:284
  91.3 318.2 %copy-start.45 = (f32[768]{0:T(1024)}, f32[768]{0:T(1024)S(1)}, u32[]{:S(2)}) copy-start(f32[768]{0:T(1024)S(1)} %mul.384) | copy-start | bytes 9220
  92.8 102.5 %copy-start.2 = (bf16[4,64,1024]{2,1,0:T(8,128)(2,1)}, bf16[4,64,1024]{2,1,0:T(8,128)(2,1)S(1)}, u32[]{:S(2)}) copy-start(bf16[4,64,1024]{2,1,0:T(8,128)(2,1)S(1)} %get-tuple-element.65.q_ref) | copy-start | bytes 1572868
  92.8 151.0 %copy-start.6 = (bf16[4,64,1024]{2,1,0:T(8,128)(2,1)}, bf16[4,64,1024]{2,1,0:T(8,128)(2,1)S(1)}, u32[]{:S(2)}) copy-start(bf16[4,64,1024]{2,1,0:T(8,128)(2,1)S(1)} %get-tuple-element.64.q_ref) | copy-start | bytes 1572868
  162.1 2.2 copy-start.10
  243.7 2.2 copy-start.12
  325.4 2.2 copy-start.11
  363.7 1.7 copy-start.15
  363.7 45.9 %copy-start.41 = (f32[1024]{0:T(1024)}, f32[1024]{0:T(1024)S(1)}, u32[]{:S(2)}) copy-start(f32[1024]{0:T(1024)S(1)} %broadcast_multiply_fusion.5) | copy-start | bytes 12292
  365.7 43.9 %copy-start.47 = (f32[1024]{0:T(1024)}, f32[1024]{0:T(1024)S(1)}, u32[]{:S(2)}) copy-start(f32[1024]{0:T(1024)S(1)} %add_rsqrt_fusion) | copy-start | bytes 12292
  396.4 7.7 copy-start.16
  396.4 7.7 copy-start.51
  404.1 5.5 copy-start.27
  404.1 5.5 copy-start.28
  409.6 2.6 copy-start.52
  412.2 1.7 copy-start.19
  464.4 156.6 %reduce-scatter.6.cloned.1.call-start = ((), (), s32[]{:S(2)}) async-start(), calls=%async_computation.9 | async-start | bytes 5242880 | tf_op jit(solution)/shard_map/reduce_scatter | solution.py:284
  515.2 185.3 %reduce-scatter.8.cloned.1.call-start = ((), (), s32[]{:S(2)}) async-start(), calls=%async_computation.10 | async-start | bytes 5242880 | tf_op jit(solution)/shard_map/reduce_scatter | solution.py:284
  565.8 211.2 %reduce-scatter.14.cloned.1.call-start = ((), (), s32[]{:S(2)}) async-start(), calls=%async_computation.13 | async-start | bytes 8110080 | tf_op jit(solution)/shard_map/reduce_scatter | solution.py:263
  565.8 3.5 copy-start.31
  568.8 1.9 copy-start.20
  568.8 3.3 slice-start
  568.8 3.4 slice-start.1
  570.7 3.0 slice-start.2
  575.1 3.7 copy-start.17
  575.1 3.7 copy-start.42
  575.1 3.7 copy-start.46
  575.1 3.7 copy-start.48
  586.6 2.2 copy-start.1
  586.6 233.8 %reduce-scatter.12.cloned.1.call-start = ((), (), s32[]{:S(2)}) async-start(), calls=%async_computation.12 | async-start | bytes 4423680 | tf_op jit(solution)/shard_map/reduce_scatter | solution.py:263
  622.4 79.6 %copy-start.33 = (f32[32,1024]{1,0:T(8,128)S(1)}, f32[32,1024]{1,0:T(8,128)}, u32[]{:S(2)}) copy-start(f32[32,1024]{1,0:T(8,128)} %copy-done.32) | copy-start | bytes 393220
  622.4 79.6 %copy-start.35 = (f32[32,1024]{1,0:T(8,128)S(1)}, f32[32,1024]{1,0:T(8,128)}, u32[]{:S(2)}) copy-start(f32[32,1024]{1,0:T(8,128)} %get-tuple-element.75) | copy-start | bytes 393220
  622.4 79.6 %copy-start.36 = (f32[32,1024]{1,0:T(8,128)S(1)}, f32[32,1024]{1,0:T(8,128)}, u32[]{:S(2)}) copy-start(f32[32,1024]{1,0:T(8,128)} %get-tuple-element.76) | copy-start | bytes 393220
  622.4 79.6 %copy-start.37 = (f32[32,1024]{1,0:T(8,128)S(1)}, f32[32,1024]{1,0:T(8,128)}, u32[]{:S(2)}) copy-start(f32[32,1024]{1,0:T(8,128)} %get-tuple-element.79) | copy-start | bytes 393220
  705.1 1.1 copy-start.23
  705.3 1.6 copy-start.25
  705.5 1.9 copy-start.26
  706.3 1.9 copy-start.30
  713.5 2.4 copy-start.18
  740.5 79.9 %copy-start.14 = (bf16[4,192,1024]{2,1,0:T(8,128)(2,1)S(1)}, bf16[4,192,1024]{2,1,0:T(8,128)(2,1)}, u32[]{:S(2)}) copy-start(bf16[4,192,1024]{2,1,0:T(8,128)(2,1)} %copy-done.13) | copy-start | bytes 4718596
  740.5 79.9 %copy-start.24 = (bf16[12,64,1024]{2,1,0:T(8,128)(2,1)S(1)}, bf16[12,64,1024]{2,1,0:T(8,128)(2,1)}, u32[]{:S(2)}) copy-start(bf16[12,64,1024]{2,1,0:T(8,128)(2,1)} %copy-done.23) | copy-start | bytes 4718596
  740.5 79.9 %copy-start.40 = (f32[1024]{0:T(1024)S(1)}, f32[1024]{0:T(1024)}, u32[]{:S(2)}) copy-start(f32[1024]{0:T(1024)} %copy-done.39) | copy-start | bytes 12292
  740.5 79.9 %copy-start.44 = (f32[1024]{0:T(1024)S(1)}, f32[1024]{0:T(1024)}, u32[]{:S(2)}) copy-start(f32[1024]{0:T(1024)} %copy-done.43) | copy-start | bytes 12292
  740.5 106.7 %all-to-all-start.1 = ((bf16[4,2,98304]{2,1,0:T(2,128)(2,1)}), bf16[4,2,98304]{2,1,0:T(2,128)(2,1)}, u32[]{:S(2)}, u32[]{:S(2)}) async-start(bf16[4,2,98304]{2,1,0:T(2,128)(2,1)} %reshape.474), calls=%async_computation.1 | async-start | bytes 3145728 | tf_op jit(solution)/shard_map/all_to_all | solution.py:244
  745.1 192.4 %all-reduce.3.cloned.1.call-start = ((), (), s32[]{:S(2)}) async-start(), calls=%async_computation.21 | async-start | bytes 5013504 | tf_op jit(solution)/shard_map/psum | solution.py:264
  820.4 8.0 copy-start.21
  843.1 8.5 copy-start.50
  847.3 60.0 %all-to-all-start.3 = ((bf16[4,2,98304]{2,1,0:T(2,128)(2,1)}), bf16[4,2,98304]{2,1,0:T(2,128)(2,1)}, u32[]{:S(2)}, u32[]{:S(2)}) async-start(bf16[4,2,98304]{2,1,0:T(2,128)(2,1)} %reshape.476), calls=%async_computation.6 | async-start | bytes 3145728 | tf_op jit(solution)/shard_map/all_to_all | solution.py:296
  937.6 4.0 copy-start.22
  937.6 5.3 copy-start.34
  (11 other events, 10.5 us)
Sparse Core Ops, SparseCore 0:
  9.6 43.1 all-gather.16
  80.3 81.7 all-gather.20
  164.3 79.3 all-gather.22
  245.2 79.1 all-gather.18
  325.8 15.9 all-gather.24
  343.2 30.7 all-gather.26
  375.6 20.7 all-gather.28
  464.6 76.7 reduce-scatter.9
  543.8 77.2 reduce-scatter.5
  623.2 77.2 reduce-scatter.7
  703.3 73.6 reduce-scatter.13
  779.4 40.9 reduce-scatter.11
  824.5 113.0 all-reduce.2

commit v2 on v1

--- a/solution.py
+++ b/solution.py
@@ -11,7 +11,6 @@
 HD = 64
 EPSILON = 1e-05
 THETA_BASE = 160000.0
-GROUPS = 3
 LOG2E = math.log2(math.e)
 F32 = jnp.float32
 BF16 = jnp.bfloat16
@@ -193,15 +192,16 @@
     hidden_shard = ffn_in_weight.shape[1]
     heads = width // HD
     assert tokens.shape[0] == wa_size
-    per_group = heads // GROUPS
+    group_sizes = (heads // 3, heads // 4, heads // 4)
+    group_sizes += (heads - sum(group_sizes),)
     score_scale = 1.0 / math.sqrt(HD)
 
-    x_low = lax.all_to_all(tokens, "wa", 0, 1, tiled=True)[0]
+    x_low = lax.all_to_all(tokens, "wa", 0, 0, tiled=True).reshape(width, length)
     qkv_all = lax.all_gather(qkv_weight, "wa", axis=0)
     gains = lax.all_gather(jnp.stack([first_gain, second_gain]), "wa", axis=0)
     gains = gains.transpose(1, 0, 2).reshape(2, width, 1).astype(F32)
     gain_one, gain_two = gains[0], gains[1]
-    cot = lax.all_to_all(cotangent, "wa", 0, 1, tiled=True)[0]
+    cot = lax.all_to_all(cotangent, "wa", 0, 0, tiled=True).reshape(width, length)
     attn_mat = lax.all_gather(attn_out_weight, "wa", axis=0).reshape(width, width)
     ffn_in_mat = lax.all_gather(ffn_in_weight, "wa", axis=0).reshape(-1, width)
     ffn_out_mat = lax.all_gather(ffn_out_weight, "wa", axis=0).reshape(-1, width)
@@ -224,8 +224,9 @@
     values_own = by_head(2).astype(BF16)
 
     parts = []
-    for group in range(GROUPS):
-        rows = slice(group * per_group, (group + 1) * per_group)
+    for group, size in enumerate(group_sizes):
+        first = sum(group_sizes[:group])
+        rows = slice(first, first + size)
         kv_all = lax.all_gather(jnp.stack([keys_own[rows], values_own[rows]]), "ctx", axis=0)
         parts.append((rows, kv_all))
     results = [attend(queries[rows], kv_all) for rows, kv_all in parts]
@@ -241,7 +242,7 @@
     gelu = gate * cdf
     hidden = (gelu * up).astype(BF16).reshape(-1, length)
     output_all = (middle + dot(ffn_out_mat, hidden, 0, 0)).astype(BF16)
-    output = lax.all_to_all(output_all[None], "wa", 1, 0, tiled=True)
+    output = lax.all_to_all(output_all.reshape(tokens.shape), "wa", 0, 0, tiled=True)
 
     grad_ffn_out = dot(hidden, cot, 1, 1)
     grad_hidden = dot(ffn_out_mat, cot, 1, 0).reshape(gate.shape)
@@ -259,11 +260,7 @@
     grad_attn_out = dot(attended_low, grad_middle_low, 1, 1)
     grad_attended = dot(attn_mat, grad_middle_low, 1, 0).astype(BF16).reshape(heads, HD, length)
 
-    def sum_weights(grads):
-        own = lax.psum_scatter(grads.astype(BF16), "wa", scatter_dimension=0)
-        return lax.psum(own, ("ctx", "seq")).astype(F32)
-
-    early = sum_weights(
+    early_own = lax.psum_scatter(
         jnp.concatenate(
             [
                 grad_ffn_in.astype(BF16).reshape(wa_size, -1, width),
@@ -271,17 +268,27 @@
                 grad_attn_out.astype(BF16).reshape(wa_size, -1, width),
             ],
             axis=1,
-        )
-    )
+        ),
+        "wa",
+        scatter_dimension=0,
+    )
+    grad_queries, grad_kv = [], []
+    for group in reversed(range(len(parts))):
+        (rows, kv_all), (out, lse) = parts[group], results[group]
+        grad_part = grad_attended[rows]
+        if group == 0:
+            grad_part, early = lax.optimization_barrier((grad_part, early))
+        grad_q, grad_kv_all = attend_back(queries[rows], kv_all, grad_part, out, lse)
+        if group == len(parts) - 1:
+            early_own, grad_q = lax.optimization_barrier((early_own, grad_q))
+            early = lax.psum(early_own, ("ctx", "seq"))
+        grad_queries.append(grad_q)
+        grad_kv.append(lax.psum_scatter(grad_kv_all, "ctx", scatter_dimension=0))
+    early = early.astype(F32)
     grad_ffn_in_own = early[: 2 * hidden_shard].reshape(2, hidden_shard, width)
     grad_ffn_out_own = early[2 * hidden_shard : 3 * hidden_shard]
     grad_attn_out_own = early[3 * hidden_shard :]
-
-    grad_queries, grad_kv = [], []
-    for (rows, kv_all), (out, lse) in zip(parts, results):
-        grad_q, grad_kv_all = attend_back(queries[rows], kv_all, grad_attended[rows], out, lse)
-        grad_queries.append(grad_q)
-        grad_kv.append(lax.psum_scatter(grad_kv_all, "ctx", scatter_dimension=0))
+    grad_queries, grad_kv = grad_queries[::-1], grad_kv[::-1]
     grad_q = jnp.concatenate(grad_queries, axis=0)
     grad_k = jnp.concatenate([g[0] for g in grad_kv], axis=0).astype(F32)
     grad_v = jnp.concatenate([g[1] for g in grad_kv], axis=0)
@@ -293,11 +300,22 @@
     grad_normed_one = dot(qkv_mat, grad_projected, 0, 0)
     gain_one_grad = jnp.sum(grad_normed_one * hat_one, axis=1)
     grad_x = grad_middle + norm_back(grad_normed_one * gain_one, hat_one, inv_one)
-    grad_tokens = lax.all_to_all(grad_x.astype(BF16)[None], "wa", 1, 0, tiled=True).astype(F32)
+    grad_tokens = lax.all_to_all(
+        grad_x.astype(BF16).reshape(tokens.shape), "wa", 0, 0, tiled=True
+    ).astype(F32)
     grad_qkv = dot(grad_projected, normed_one, 1, 1)
-    grad_qkv_own = sum_weights(grad_qkv.reshape(wa_size, -1, width)).reshape(3, shard, width)
-    gain_sums = lax.psum(jnp.stack([gain_one_grad, gain_two_grad]), ("ctx", "seq", "wa"))
-    gain_own = lax.dynamic_slice_in_dim(gain_sums, lax.axis_index("wa") * shard, shard, 1)
+    gain_rows = jnp.stack([gain_one_grad, gain_two_grad]).reshape(2, wa_size, shard)
+    gain_rows = jnp.pad(gain_rows.transpose(1, 0, 2), ((0, 0), (0, 14), (0, width - shard)))
+    late_own = lax.psum_scatter(
+        jnp.concatenate(
+            [grad_qkv.astype(BF16).reshape(wa_size, -1, width), gain_rows.astype(BF16)], axis=1
+        ),
+        "wa",
+        scatter_dimension=0,
+    )
+    late = lax.psum(late_own, ("ctx", "seq")).astype(F32)
+    grad_qkv_own = late[: 3 * shard].reshape(3, shard, width)
+    gain_own = late[3 * shard : 3 * shard + 2, :shard]
     return (
         output,
         grad_tokens,

time: 959 us -> 1030 us (1.074)
  waiting for transfers between devices: 392 us -> 528 us
  blocking collectives: 81.4 us -> 31.3 us
  local copies, waits for them, and re-layouts: 88 us -> 72.6 us
    reduce_scatter x3 -> x4, waiting for transfers between devices: 108 us -> 188 us  [local(): grad_kv.append(lax.psum_scatter(grad_kv_all, 'ctx', scatter_dimension=0))]
    psum x1 -> x2, waiting for transfers between devices: 24.8 us -> 75.6 us  [the longest x1 62 us: local(): late = lax.psum(late_own, ('ctx', 'seq')).astype(F32)]
    psum x1 -> x0, blocking collectives: 50.1 us -> none  [local(): lax.psum(jnp.stack([gain_one_grad, gain_two_grad]), ('ctx', 'seq', 'wa'))]
    reduce_scatter x2, waiting for transfers between devices: 75.2 us -> 37.9 us  [the longest x1 30.7 us: local(): lax.psum_scatter(jnp.concatenate([grad_ffn_in.astype(BF16).reshape(wa_siz...]
    all_to_all x4, waiting for transfers between devices: 0.01 us -> 36.7 us  [the longest x1 25.5 us: local(): lax.all_to_all(output_all.reshape(tokens.shape), 'wa', 0, 0, tiled=True)]
    unnamed x4 -> x1, other arithmetic: 22.4 us -> 0.01 us
    unnamed x126 -> x110, local copies, waits for them, and re-layouts: 44 us -> 24.6 us
    all_gather x3 -> x4, waiting for transfers between devices: 166 us -> 174 us  [local(): lax.all_gather(jnp.stack([keys_own[rows], values_own[rows]]), 'ctx', axis=0)]
  transfers between devices with their start and end apart: 17 -> 20, of which waited for: 11 -> 15; matrix products, arithmetic and copies ran while one was open for 14% -> 8% of each run, Pallas kernels for 20% -> 23%
where the time goes in v2:
time: 1030 us; the launch traced here: 1020 us
  waiting for transfers between devices  528 us (51%)
  Pallas kernels  239 us (23%)
  matrix products  73.5 us (7%)
  local copies, waits for them, and re-layouts  72.6 us (7%)
  other arithmetic  45 us (4%)
  blocking collectives  31.3 us (3%)
  starting transfers between devices  17.8 us (2%)
  between operations  14.8 us (1%)
    reduce_scatter x4, waiting for transfers between devices, local(): grad_kv.append(lax.psum_scatter(grad_kv_all, 'ctx', scatter_dimension=0))  188 us
    all_gather x4, waiting for transfers between devices, local(): lax.all_gather(jnp.stack([keys_own[rows], values_own[rows]]), 'ctx', axis=0)  174 us
    pallas_call x4, Pallas kernels, attend_back(): pl.pallas_call(functools.partial(backward_kernel, key_tile=math.gcd(key_l...  147 us
    pallas_call x4, Pallas kernels, attend(): pl.pallas_call(functools.partial(forward_kernel, key_tile=math.gcd(key_le...  92.4 us
    dot_general x12, matrix products, dot(): lax.dot_general(a, b, (((contract_a,), (contract_b,)), ((), ())), preferr...  73.5 us
    psum x1, waiting for transfers between devices, local(): late = lax.psum(late_own, ('ctx', 'seq')).astype(F32)  62 us
    all_gather x1, blocking collectives, local(): gains = lax.all_gather(jnp.stack([first_gain, second_gain]), 'wa', axis=0)  31.3 us
    reduce_scatter x1, waiting for transfers between devices, local(): lax.psum_scatter(jnp.concatenate([grad_ffn_in.astype(BF16).reshape(wa_siz...  30.7 us
  transfers between devices with their start and end apart: 20, of which 15 were waited for; matrix products, arithmetic and copies ran while one was open for 8% of the time, Pallas kernels for 23%

profile of v2, /device:TPU:0, one launch (start us, length us, event | category | flops | bytes accessed | tf_op | source)
XLA Modules:
  0.0 1021.6 jit_solution(8492253025388780558)
XLA Ops:
  7.9 4.2 all-to-all-start
  12.2 31.3 %all-gather.9 = bf16[4,2,192]{2,1,0:T(2,128)(2,1)S(1)} all-gather(bf16[1,2,192]{2,1,0:T(2,128)(2,1)S(1)} %maximum_bitcast_fusion.1), channel_id=2, replica_groups=mesh['ctx'=4,'seq'=2,'wa'=4] {'wa'}, dimensions={0}, use_global_device_ids=true | all-gather | bytes 3840 | tf_op jit(solution)/shard_map/all_gather | solution.py:201
  47.4 5.4 all-gather.19.cloned.1.call-done
  52.8 8.3 convolution_bitcast_fusion.1
  61.1 9.6 copy.35
  70.7 5.3 fusion.59
  76.0 2.1 slice.360
  81.6 2.0 pad_maximum_fusion.7
  86.2 4.4 all-to-all-start.2
  92.0 2.4 subtract_convert_fusion.3
  94.5 32.3 %all-gather.27.cloned.1.call-done = bf16[8,2,64,1024]{3,2,1,0:T(8,128)(2,1)} async-done(((bf16[2,2,64,1024]{3,2,1,0:T(8,128)(2,1)}), bf16[8,2,64,1024]{3,2,1,0:T(8,128)(2,1)}) %all-gather.27.cloned.1.call-update) | async-done | bytes 2097168 | tf_op jit(solution)/shard_map/all_gather | solution.py:230
  128.4 15.4 %shard_map.146 = (f32[2,64,1024]{2,1,0:T(8,128)S(1)}, f32[2,1,1024]{2,1,0:T(1,128)S(1)}) custom-call(bf16[2,64,1024]{2,1,0:T(8,128)(2,1)S(1)} %pad_maximum_fusion.11.q_ref, bf16[4,2,2,64,1024]{4,3,2,1,0:T(8,128)(2,1)S(1)} %bitcast.238), custom_call_target="tpu_custom_call" | custom-call | flops 8589934592 | bytes 4194304 | tf_op jit(solution)/shard_map/pallas_call | solution.py:88
  144.5 46.7 %all-gather.25.cloned.1.call-done = bf16[8,3,64,1024]{3,2,1,0:T(8,128)(2,1)} async-done(((bf16[2,3,64,1024]{3,2,1,0:T(8,128)(2,1)}), bf16[8,3,64,1024]{3,2,1,0:T(8,128)(2,1)}) %all-gather.25.cloned.1.call-update) | async-done | bytes 3145744 | tf_op jit(solution)/shard_map/all_gather | solution.py:230
  191.2 1.9 copy-done.16
  193.1 23.1 %shard_map.145 = (f32[3,64,1024]{2,1,0:T(8,128)S(1)}, f32[3,1,1024]{2,1,0:T(1,128)S(1)}) custom-call(bf16[3,64,1024]{2,1,0:T(8,128)(2,1)S(1)} %get-tuple-element.75.q_ref, bf16[4,2,3,64,1024]{4,3,2,1,0:T(8,128)(2,1)S(1)} %bitcast.237), custom_call_target="tpu_custom_call" | custom-call | flops 12884901888 | bytes 6291456 | tf_op jit(solution)/shard_map/pallas_call | solution.py:88
  216.2 38.6 %all-gather.23.cloned.1.call-done = bf16[8,3,64,1024]{3,2,1,0:T(8,128)(2,1)} async-done(((bf16[2,3,64,1024]{3,2,1,0:T(8,128)(2,1)}), bf16[8,3,64,1024]{3,2,1,0:T(8,128)(2,1)}) %all-gather.23.cloned.1.call-update) | async-done | bytes 3145744 | tf_op jit(solution)/shard_map/all_gather | solution.py:230
  254.8 1.9 copy-done.15
  256.7 23.1 %shard_map.144 = (f32[3,64,1024]{2,1,0:T(8,128)S(1)}, f32[3,1,1024]{2,1,0:T(1,128)S(1)}) custom-call(bf16[3,64,1024]{2,1,0:T(8,128)(2,1)S(1)} %get-tuple-element.74.q_ref, bf16[4,2,3,64,1024]{4,3,2,1,0:T(8,128)(2,1)S(1)} %bitcast.235), custom_call_target="tpu_custom_call" | custom-call | flops 12884901888 | bytes 6291456 | tf_op jit(solution)/shard_map/pallas_call | solution.py:88
  279.8 56.5 %all-gather.21.cloned.1.call-done = bf16[8,4,64,1024]{3,2,1,0:T(8,128)(2,1)} async-done(((bf16[2,4,64,1024]{3,2,1,0:T(8,128)(2,1)}), bf16[8,4,64,1024]{3,2,1,0:T(8,128)(2,1)}) %all-gather.21.cloned.1.call-update) | async-done | bytes 4194320 | tf_op jit(solution)/shard_map/all_gather | solution.py:230
  336.3 2.2 copy-done.14
  338.5 30.9 %shard_map.143 = (f32[4,64,1024]{2,1,0:T(8,128)S(1)}, f32[4,1,1024]{2,1,0:T(1,128)S(1)}) custom-call(bf16[4,64,1024]{2,1,0:T(8,128)(2,1)S(1)} %fusion.43.q_ref, bf16[4,2,4,64,1024]{4,3,2,1,0:T(8,128)(2,1)S(1)} %bitcast.233), custom_call_target="tpu_custom_call" | custom-call | flops 17179869184 | bytes 8388608 | tf_op jit(solution)/shard_map/pallas_call | solution.py:88
  371.8 5.4 fusion.62
  377.2 2.3 multiply_reduce_fusion.1
  379.5 6.6 all-gather.31.cloned.1.call-done
  386.1 10.7 %convolution_bitcast_fusion = f32[2304,1024]{0,1:T(8,128)} fusion(bf16[2304,768]{1,0:T(8,128)(2,1)} %bitcast.278, f32[768,1024]{1,0:T(8,128)} %get-tuple-element.95, f32[768]{0:T(1024)S(1)} %mul.378, f32[1024]{0:T(1024)S(1)} %add_rsqrt_fusion, f32[1024]{0:T(1024)S(1)} %broadcast_multiply_fusion.5), kind=kOutput, calls=%fused_computation.5 | convolution fusion | flops 3627024384 | bytes 16133120 | tf_op jit(solution)/shard_map/dot_general | solution.py:20
  396.8 9.6 copy.36
  406.5 5.5 fusion.8
  412.0 7.1 fusion.6
  421.2 7.0 fusion.17
  428.1 3.4 multiply_add_fusion
  431.6 1.8 copy-done.21
  435.3 6.4 convolution_convert_fusion.1
  441.7 3.4 convolution_convert_fusion.2
  445.2 3.2 pad_maximum_fusion
  448.5 3.8 fusion.38
  453.4 24.2 %shard_map.147 = (f32[2,64,1024]{2,1,0:T(8,128)S(1)}, bf16[4,2,2,64,1024]{4,3,2,1,0:T(8,128)(2,1)}) custom-call(bf16[2,64,1024]{2,1,0:T(8,128)(2,1)S(1)} %copy-done.13, bf16[4,2,2,64,1024]{4,3,2,1,0:T(8,128)(2,1)S(1)} %bitcast.239, bf16[2,64,1024]{2,1,0:T(8,128)(2,1)S(1)} %bitcast.231, f32[2,64,1024]{2,1,0:T(8,128)S(1)} %get-tuple-element.31.out_ref, ...), custom_call_target="tpu_custom_call" | custom-call | flops 21474836480 | bytes 8388608 | tf_op jit(solution)/shard_map/pallas_call | solution.py:156
  477.6 30.7 %reduce-scatter.7.cloned.1.call-done = bf16[1,1056,768]{2,1,0:T(8,128)(2,1)} async-done(((bf16[4,1056,768]{2,1,0:T(8,128)(2,1)}), bf16[1,1056,768]{2,1,0:T(8,128)(2,1)}) %reduce-scatter.7.cloned.1.call-update) | async-done | bytes 1622032 | tf_op jit(solution)/shard_map/reduce_scatter | solution.py:263
  509.1 1.9 fusion.60
  511.1 36.8 %shard_map.150 = (f32[3,64,1024]{2,1,0:T(8,128)S(1)}, bf16[4,2,3,64,1024]{4,3,2,1,0:T(8,128)(2,1)}) custom-call(bf16[3,64,1024]{2,1,0:T(8,128)(2,1)S(1)} %copy-done.10, bf16[4,2,3,64,1024]{4,3,2,1,0:T(8,128)(2,1)} %bitcast.236, bf16[3,64,1024]{2,1,0:T(8,128)(2,1)S(1)} %bitcast.230, f32[3,64,1024]{2,1,0:T(8,128)S(1)} %get-tuple-element.30.out_ref, ...), custom_call_target="tpu_custom_call" | custom-call | flops 32212254720 | bytes 12582912 | tf_op jit(solution)/shard_map/pallas_call | solution.py:156
  549.0 37.3 %shard_map.149 = (f32[3,64,1024]{2,1,0:T(8,128)S(1)}, bf16[4,2,3,64,1024]{4,3,2,1,0:T(8,128)(2,1)}) custom-call(bf16[3,64,1024]{2,1,0:T(8,128)(2,1)S(1)} %copy-done.8, bf16[4,2,3,64,1024]{4,3,2,1,0:T(8,128)(2,1)} %bitcast.234, bf16[3,64,1024]{2,1,0:T(8,128)(2,1)S(1)} %bitcast.229, f32[3,64,1024]{2,1,0:T(8,128)S(1)} %get-tuple-element.29.out_ref, ...), custom_call_target="tpu_custom_call" | custom-call | flops 32212254720 | bytes 12582912 | tf_op jit(solution)/shard_map/pallas_call | solution.py:156
  587.2 1.9 slice.241
  589.2 13.6 %all-reduce.4.cloned.1.call-done = bf16[1056,768]{1,0:T(8,128)(2,1)} async-done(((bf16[1056,768]{1,0:T(8,128)(2,1)}), bf16[1056,768]{1,0:T(8,128)(2,1)}) %all-reduce.4.cloned.1.call-update) | async-done | bytes 1622032 | tf_op jit(solution)/shard_map/psum | solution.py:284
  604.9 48.4 %shard_map.148 = (f32[4,64,1024]{2,1,0:T(8,128)S(1)}, bf16[4,2,4,64,1024]{4,3,2,1,0:T(8,128)(2,1)}) custom-call(bf16[4,64,1024]{2,1,0:T(8,128)(2,1)S(1)} %copy-done.6, bf16[4,2,4,64,1024]{4,3,2,1,0:T(8,128)(2,1)} %bitcast.232, bf16[4,64,1024]{2,1,0:T(8,128)(2,1)S(1)} %bitcast.228, f32[4,64,1024]{2,1,0:T(8,128)S(1)} %copy-done.1, ...), custom_call_target="tpu_custom_call" | custom-call | flops 42949672960 | bytes 16777216 | tf_op jit(solution)/shard_map/pallas_call | solution.py:156
  654.1 1.9 slice_bitcast_fusion.10
  656.1 54.3 %reduce-scatter.13.cloned.1.call-done = bf16[1,2,3,64,1024]{4,3,2,1,0:T(8,128)(2,1)} async-done(((bf16[4,2,3,64,1024]{4,3,2,1,0:T(8,128)(2,1)}), bf16[1,2,3,64,1024]{4,3,2,1,0:T(8,128)(2,1)}) %reduce-scatter.13.cloned.1.call-update) | async-done | bytes 786448 | tf_op jit(solution)/shard_map/reduce_scatter | solution.py:286
  710.4 2.1 slice_bitcast_fusion.5
  712.4 60.5 %reduce-scatter.11.cloned.1.call-done = bf16[1,2,3,64,1024]{4,3,2,1,0:T(8,128)(2,1)} async-done(((bf16[4,2,3,64,1024]{4,3,2,1,0:T(8,128)(2,1)}), bf16[1,2,3,64,1024]{4,3,2,1,0:T(8,128)(2,1)}) %reduce-scatter.11.cloned.1.call-update) | async-done | bytes 786448 | tf_op jit(solution)/shard_map/reduce_scatter | solution.py:286
  773.0 2.1 slice_bitcast_fusion.6
  778.9 73.1 %reduce-scatter.9.cloned.1.call-done = bf16[1,2,4,64,1024]{4,3,2,1,0:T(8,128)(2,1)} async-done(((bf16[4,2,4,64,1024]{4,3,2,1,0:T(8,128)(2,1)}), bf16[1,2,4,64,1024]{4,3,2,1,0:T(8,128)(2,1)}) %reduce-scatter.9.cloned.1.call-update) | async-done | bytes 1048592 | tf_op jit(solution)/shard_map/reduce_scatter | solution.py:286
  853.6 2.9 subtract_convert_fusion
  858.0 2.9 pad_maximum_fusion.1
  862.2 5.9 fusion.18
  868.2 6.7 convolution_convert_fusion
  874.9 2.1 fusion.15
  877.0 7.3 fusion.16
  884.4 3.6 all-to-all-start.1
  888.1 5.1 fusion.31
  893.1 25.5 %all-to-all-done.1 = bf16[4,192,1024]{2,1,0:T(8,128)(2,1)S(1)} async-done(((bf16[4,192,1024]{2,1,0:T(8,128)(2,1)}), bf16[4,192,1024]{2,1,0:T(8,128)(2,1)S(1)}, u32[]{:S(2)}, u32[]{:S(2)}) %all-to-all-start.1) | async-done | bytes 1572896 | tf_op jit(solution)/shard_map/all_to_all | solution.py:245
  918.6 4.4 all-to-all-start.3
  923.0 7.1 reduce-scatter.17.cloned.1.call-done
  933.3 11.2 %all-to-all-done.3 = bf16[4,192,1024]{2,1,0:T(8,128)(2,1)} async-done(((bf16[4,192,1024]{2,1,0:T(8,128)(2,1)}), bf16[4,192,1024]{2,1,0:T(8,128)(2,1)}, u32[]{:S(2)}, u32[]{:S(2)}) %all-to-all-start.3) | async-done | bytes 1572896 | tf_op jit(solution)/shard_map/all_to_all | solution.py:303
  944.5 3.5 convert_element_type.176
  948.0 62.0 %all-reduce.6.cloned.1.call-done = bf16[592,768]{1,0:T(8,128)(2,1)} async-done(((bf16[592,768]{1,0:T(8,128)(2,1)}), bf16[592,768]{1,0:T(8,128)(2,1)}) %all-reduce.6.cloned.1.call-update) | async-done | bytes 909328 | tf_op jit(solution)/shard_map/psum | solution.py:316
  1011.3 2.5 slice.258
  (199 shorter events, 41.5 us)
Async XLA Ops:
  7.2 5.0 copy-start.50
  7.2 5.0 copy-start.51
  7.2 45.6 %all-gather.19.cloned.1.call-start = ((), (), s32[]{:S(2)}) async-start(), calls=%async_computation.18 | async-start | bytes 4423680 | tf_op jit(solution)/shard_map/all_gather | solution.py:200
  7.9 37.6 %all-to-all-start = ((bf16[4,192,1024]{2,1,0:T(8,128)(2,1)}), bf16[4,192,1024]{2,1,0:T(8,128)(2,1)S(1)}, u32[]{:S(2)}, u32[]{:S(2)}) async-start(bf16[4,192,1024]{2,1,0:T(8,128)(2,1)} %param.8), calls=%async_computation | async-start | bytes 3145728 | tf_op jit(solution)/shard_map/all_to_all | solution.py:199
  12.2 114.6 %all-gather.27.cloned.1.call-start = ((), (), s32[]{:S(2)}) async-start(), calls=%async_computation.22 | async-start | bytes 2621440 | tf_op jit(solution)/shard_map/all_gather | solution.py:230
  45.5 32.7 %copy-start.32 = (f32[32,1024]{1,0:T(8,128)}, f32[32,1024]{1,0:T(8,128)S(1)}, u32[]{:S(2)}) copy-start(f32[32,1024]{1,0:T(8,128)S(1)} %get-tuple-element.93) | copy-start | bytes 393220
  45.5 15.6 %copy-start.19 = (bf16[4,192,1024]{2,1,0:T(8,128)(2,1)}, bf16[4,192,1024]{2,1,0:T(8,128)(2,1)S(1)}, u32[]{:S(2)}) copy-start(bf16[4,192,1024]{2,1,0:T(8,128)(2,1)S(1)} %all-to-all-done) | copy-start | bytes 4718596
  47.4 13.8 %copy-start.24 = (bf16[4,192,1024]{2,1,0:T(8,128)(2,1)}, bf16[4,192,1024]{2,1,0:T(8,128)(2,1)S(1)}, u32[]{:S(2)}) copy-start(bf16[4,192,1024]{2,1,0:T(8,128)(2,1)S(1)} %fusion.23) | copy-start | bytes 4718596
  79.6 111.5 %all-gather.25.cloned.1.call-start = ((), (), s32[]{:S(2)}) async-start(), calls=%async_computation.21 | async-start | bytes 3932160 | tf_op jit(solution)/shard_map/all_gather | solution.py:230
  81.5 173.2 %all-gather.23.cloned.1.call-start = ((), (), s32[]{:S(2)}) async-start(), calls=%async_computation.20 | async-start | bytes 3932160 | tf_op jit(solution)/shard_map/all_gather | solution.py:230
  83.6 252.7 %all-gather.21.cloned.1.call-start = ((), (), s32[]{:S(2)}) async-start(), calls=%async_computation.19 | async-start | bytes 5242880 | tf_op jit(solution)/shard_map/all_gather | solution.py:230
  84.8 7.1 copy-start.40
  84.8 7.1 copy-start.41
  84.8 287.0 %all-gather.29.cloned.1.call-start = ((), (), s32[]{:S(2)}) async-start(), calls=%async_computation.23 | async-start | bytes 1474560 | tf_op jit(solution)/shard_map/all_gather | solution.py:205
  85.4 300.7 %all-gather.31.cloned.1.call-start = ((), (), s32[]{:S(2)}) async-start(), calls=%async_computation.24 | async-start | bytes 4423680 | tf_op jit(solution)/shard_map/all_gather | solution.py:206
  86.2 325.9 %all-to-all-start.2 = ((bf16[4,192,1024]{2,1,0:T(8,128)(2,1)}), bf16[4,192,1024]{2,1,0:T(8,128)(2,1)}, u32[]{:S(2)}, u32[]{:S(2)}) async-start(bf16[4,192,1024]{2,1,0:T(8,128)(2,1)} %param.15), calls=%async_computation.2 | async-start | bytes 3145728 | tf_op jit(solution)/shard_map/all_to_all | solution.py:204
  90.5 321.5 %all-gather.33.cloned.1.call-start = ((), (), s32[]{:S(2)}) async-start(), calls=%async_computation.25 | async-start | bytes 2211840 | tf_op jit(solution)/shard_map/all_gather | solution.py:207
  91.3 417.0 %reduce-scatter.7.cloned.1.call-start = ((), (), s32[]{:S(2)}) async-start(), calls=%async_computation.10 | async-start | bytes 8110080 | tf_op jit(solution)/shard_map/reduce_scatter | solution.py:263
  94.3 49.4 %copy-start.12 = (bf16[2,64,1024]{2,1,0:T(8,128)(2,1)}, bf16[2,64,1024]{2,1,0:T(8,128)(2,1)S(1)}, u32[]{:S(2)}) copy-start(bf16[2,64,1024]{2,1,0:T(8,128)(2,1)S(1)} %pad_maximum_fusion.11.q_ref) | copy-start | bytes 786436
  94.4 96.8 %copy-start.9 = (bf16[3,64,1024]{2,1,0:T(8,128)(2,1)}, bf16[3,64,1024]{2,1,0:T(8,128)(2,1)S(1)}, u32[]{:S(2)}) copy-start(bf16[3,64,1024]{2,1,0:T(8,128)(2,1)S(1)} %get-tuple-element.75.q_ref) | copy-start | bytes 1179652
  94.4 160.4 %copy-start.7 = (bf16[3,64,1024]{2,1,0:T(8,128)(2,1)}, bf16[3,64,1024]{2,1,0:T(8,128)(2,1)S(1)}, u32[]{:S(2)}) copy-start(bf16[3,64,1024]{2,1,0:T(8,128)(2,1)S(1)} %get-tuple-element.74.q_ref) | copy-start | bytes 1179652
  94.5 241.8 %copy-start.5 = (bf16[4,64,1024]{2,1,0:T(8,128)(2,1)}, bf16[4,64,1024]{2,1,0:T(8,128)(2,1)S(1)}, u32[]{:S(2)}) copy-start(bf16[4,64,1024]{2,1,0:T(8,128)(2,1)S(1)} %fusion.43.q_ref) | copy-start | bytes 1572868
  126.8 1.6 copy-start.17
  191.2 1.9 copy-start.16
  254.8 1.9 copy-start.15
  336.3 2.2 copy-start.14
  338.5 32.0 %copy-start.34 = (bf16[2,64,1024]{2,1,0:T(8,128)(2,1)S(1)}, bf16[2,64,1024]{2,1,0:T(8,128)(2,1)}, u32[]{:S(2)}) copy-start(bf16[2,64,1024]{2,1,0:T(8,128)(2,1)} %convert_element_type.157) | copy-start | bytes 786436
  419.2 2.0 copy-start.49
  428.1 5.2 copy-start.27
  431.6 1.8 copy-start.21
  435.3 6.4 copy-start.23
  448.4 5.0 copy-start.13
  448.4 154.3 %all-reduce.4.cloned.1.call-start = ((), (), s32[]{:S(2)}) async-start(), calls=%async_computation.11 | async-start | bytes 3244032 | tf_op jit(solution)/shard_map/psum | solution.py:284
  448.5 4.9 copy-start.18
  452.3 1.1 copy-start.26
  477.6 33.5 %copy-start.10 = (bf16[3,64,1024]{2,1,0:T(8,128)(2,1)S(1)}, bf16[3,64,1024]{2,1,0:T(8,128)(2,1)}, u32[]{:S(2)}) copy-start(bf16[3,64,1024]{2,1,0:T(8,128)(2,1)} %copy-done.9) | copy-start | bytes 1179652
  508.4 145.8 %reduce-scatter.15.cloned.1.call-start = ((), (), s32[]{:S(2)}) async-start(), calls=%async_computation.15 | async-start | bytes 2621440 | tf_op jit(solution)/shard_map/reduce_scatter | solution.py:286
  509.1 201.3 %reduce-scatter.13.cloned.1.call-start = ((), (), s32[]{:S(2)}) async-start(), calls=%async_computation.14 | async-start | bytes 3932160 | tf_op jit(solution)/shard_map/reduce_scatter | solution.py:286
  547.9 1.1 copy-start.11
  547.9 225.1 %reduce-scatter.11.cloned.1.call-start = ((), (), s32[]{:S(2)}) async-start(), calls=%async_computation.13 | async-start | bytes 3932160 | tf_op jit(solution)/shard_map/reduce_scatter | solution.py:286
  587.1 15.6 %copy-start.1 = (f32[4,64,1024]{2,1,0:T(8,128)S(1)}, f32[4,64,1024]{2,1,0:T(8,128)}, u32[]{:S(2)}) copy-start(f32[4,64,1024]{2,1,0:T(8,128)} %copy-done) | copy-start | bytes 3145732
  587.2 264.8 %reduce-scatter.9.cloned.1.call-start = ((), (), s32[]{:S(2)}) async-start(), calls=%async_computation.12 | async-start | bytes 5242880 | tf_op jit(solution)/shard_map/reduce_scatter | solution.py:286
  602.8 1.0 copy-start.4
  603.8 1.0 copy-start.6
  653.3 276.9 %reduce-scatter.17.cloned.1.call-start = ((), (), s32[]{:S(2)}) async-start(), calls=%async_computation.16 | async-start | bytes 4546560 | tf_op jit(solution)/shard_map/reduce_scatter | solution.py:309
  654.1 122.0 %copy-start.3 = (f32[3,64,1024]{2,1,0:T(8,128)S(1)}, f32[3,64,1024]{2,1,0:T(8,128)}, u32[]{:S(2)}) copy-start(f32[3,64,1024]{2,1,0:T(8,128)} %copy-done.2) | copy-start | bytes 2359300
  776.1 77.1 %copy-start.30 = (bf16[3,64,1024]{2,1,0:T(8,128)(2,1)S(1)}, bf16[3,64,1024]{2,1,0:T(8,128)(2,1)}, u32[]{:S(2)}) copy-start(bf16[3,64,1024]{2,1,0:T(8,128)(2,1)} %get-tuple-element.82) | copy-start | bytes 1179652
  776.1 77.1 %copy-start.31 = (bf16[3,64,1024]{2,1,0:T(8,128)(2,1)S(1)}, bf16[3,64,1024]{2,1,0:T(8,128)(2,1)}, u32[]{:S(2)}) copy-start(bf16[3,64,1024]{2,1,0:T(8,128)(2,1)} %get-tuple-element.80) | copy-start | bytes 1179652
  776.1 77.2 %copy-start.36 = (bf16[2,64,1024]{2,1,0:T(8,128)(2,1)S(1)}, bf16[2,64,1024]{2,1,0:T(8,128)(2,1)}, u32[]{:S(2)}) copy-start(bf16[2,64,1024]{2,1,0:T(8,128)(2,1)} %get-tuple-element.84) | copy-start | bytes 786436
  778.9 74.7 %copy-start.33 = (f32[32,1024]{1,0:T(8,128)S(1)}, f32[32,1024]{1,0:T(8,128)}, u32[]{:S(2)}) copy-start(f32[32,1024]{1,0:T(8,128)} %copy-done.32) | copy-start | bytes 393220
  778.9 74.7 %copy-start.37 = (f32[32,1024]{1,0:T(8,128)S(1)}, f32[32,1024]{1,0:T(8,128)}, u32[]{:S(2)}) copy-start(f32[32,1024]{1,0:T(8,128)} %get-tuple-element.87) | copy-start | bytes 393220
  778.9 74.7 %copy-start.38 = (f32[32,1024]{1,0:T(8,128)S(1)}, f32[32,1024]{1,0:T(8,128)}, u32[]{:S(2)}) copy-start(f32[32,1024]{1,0:T(8,128)} %get-tuple-element.88) | copy-start | bytes 393220
  778.9 74.7 %copy-start.39 = (f32[32,1024]{1,0:T(8,128)S(1)}, f32[32,1024]{1,0:T(8,128)}, u32[]{:S(2)}) copy-start(f32[32,1024]{1,0:T(8,128)} %get-tuple-element.91) | copy-start | bytes 393220
  856.6 1.1 copy-start.29
  856.6 1.2 copy-start.35
  858.0 2.9 copy-start.20
  858.0 2.9 copy-start.43
  858.0 2.9 copy-start.45
  858.0 4.2 copy-start.48
  862.2 6.0 copy-start.25
  884.4 34.2 %all-to-all-start.1 = ((bf16[4,192,1024]{2,1,0:T(8,128)(2,1)}), bf16[4,192,1024]{2,1,0:T(8,128)(2,1)S(1)}, u32[]{:S(2)}, u32[]{:S(2)}) async-start(bf16[4,192,1024]{2,1,0:T(8,128)(2,1)} %bitcast.270), calls=%async_computation.1 | async-start | bytes 3145728 | tf_op jit(solution)/shard_map/all_to_all | solution.py:245
  893.1 37.1 %copy-start.22 = (bf16[1056,768]{1,0:T(8,128)(2,1)S(1)}, bf16[1056,768]{1,0:T(8,128)(2,1)}, u32[]{:S(2)}) copy-start(bf16[1056,768]{1,0:T(8,128)(2,1)} %all-reduce.4.cloned.1.call-done) | copy-start | bytes 4866052
  918.6 25.9 %all-to-all-start.3 = ((bf16[4,192,1024]{2,1,0:T(8,128)(2,1)}), bf16[4,192,1024]{2,1,0:T(8,128)(2,1)}, u32[]{:S(2)}, u32[]{:S(2)}) async-start(bf16[4,192,1024]{2,1,0:T(8,128)(2,1)} %bitcast.256), calls=%async_computation.8 | async-start | bytes 3145728 | tf_op jit(solution)/shard_map/all_to_all | solution.py:303
  923.0 87.0 %all-reduce.6.cloned.1.call-start = ((), (), s32[]{:S(2)}) async-start(), calls=%async_computation.17 | async-start | bytes 1818624 | tf_op jit(solution)/shard_map/psum | solution.py:316
  (8 other events, 6.7 us)
Sparse Core Ops, SparseCore 0:
  9.6 43.1 all-gather.18
  79.8 46.9 all-gather.26
  128.9 62.2 all-gather.24
  192.6 62.1 all-gather.22
  256.8 79.4 all-gather.20
  337.7 15.9 all-gather.28
  355.3 30.7 all-gather.30
  387.7 20.7 all-gather.32
  448.5 59.7 reduce-scatter.6
  512.2 90.5 all-reduce.3
  605.2 43.1 reduce-scatter.14
  650.6 59.7 reduce-scatter.12
  712.7 60.2 reduce-scatter.10
  775.1 76.7 reduce-scatter.8
  877.2 52.9 reduce-scatter.16
  933.5 76.4 all-reduce.5
